TPU v7x, 32 devices: a whole 2x2x4 slice. The times are simulated.
32 devices in a mesh: lat: 4 (over y, core), lon: 8 (over z, x).
Axes of the slice: x: 2, y: 2, z: 4, core: 2. Of those that a mesh axis runs over, the one named last changes fastest.
Arguments:
- field: bfloat16 [64, 512, 256], P('lat', 'lon'), may hold values from -6 to 6
- filters: bfloat16 [64, 4, 9, 264], P('lat'), may hold values from -0.1875 to 0.1875
- sector_width: int32 [8], P('lat'), may hold values from 1 to 2, as said below
- block_offset: int32 [8, 4], P('lat'), may hold values from -8 to 7, as said below
- mixing: bfloat16 [9, 32, 256], replicated, may hold values from -0.375 to 0.375
Outputs:
- output: bfloat16 [64, 512, 256], P('lat', 'lon')
Inputs may be any that keep to these rules, and one draw needn't show every extreme that they name: `sector_width`: the last row group has width 2, some row group has width 1. `block_offset`: in units of 8 longitudes; the last row group holds both ends of the range.
All inputs are finite; a program needn't handle non-finite values.
Results may differ from a plain program's by a relative error of at most 0.0049.
Values may be sent and summed in bfloat16 or wider, within the bound.
A program may use at most 128 MiB of HBM per device.

v0:
```python
import jax
import jax.numpy as jnp
from jax import lax
from jax.sharding import PartitionSpec as P

K = 9
G = 8
R = 16
RG = 8
NB = 4
BW = 8
SMAX = 2


def from_behind(value, axis, steps):
    count = lax.axis_size(axis)
    pairs = [(source, (source + steps) % count) for source in range(count)]
    return lax.ppermute(value, axis, pairs)


def extended_2(value, sides, width):
    for axis, dim in sides:
        count, length = (lax.axis_size(axis), value.shape[dim])
        up = [(i, (i + 1) % count) for i in range(count - 1)]
        down = [(j, i) for i, j in up]
        last = lax.slice_in_dim(value, length - width, length, axis=dim)
        leading = lax.slice_in_dim(value, 0, width, axis=dim)
        before = lax.ppermute(last, axis, up)
        after = lax.ppermute(leading, axis, down)
        value = jnp.concatenate([before, value, after], axis=dim)
    return value


def widen(source):
    west_sectors = []
    east_sectors = []
    for distance in range(SMAX):
        west_sectors.append(from_behind(source, "lon", distance + 1))
        east_sectors.append(from_behind(source, "lon", -(distance + 1)))
    return jnp.concatenate(west_sectors[::-1] + [source] + east_sectors, axis=1)


def on_device(field, filters, sector_width, block_offset, mixing):
    rows, lon_dev, chans = field.shape
    groups = sector_width.shape[0]
    span = 2 * R + 1
    tall_rows = RG + 2 * R
    group_chans = chans // G
    flat_field = field.reshape(rows, lon_dev * chans)
    tall = extended_2(flat_field, (("lat", 0),), R)
    extended = widen(tall)
    shifts = BW * block_offset * sector_width[:, None]
    place_p = lax.broadcasted_iota(jnp.int32, (RG, span, tall_rows), 0)
    place_r = lax.broadcasted_iota(jnp.int32, (RG, span, tall_rows), 1)
    place_a = lax.broadcasted_iota(jnp.int32, (RG, span, tall_rows), 2)
    placement = (place_a == place_p + place_r).astype(jnp.float32)
    mask_rows = lax.broadcasted_iota(jnp.int32, (chans, chans), 0) // group_chans
    mask_cols = lax.broadcasted_iota(jnp.int32, (chans, chans), 1) // group_chans
    tiled_mix = jnp.tile(mixing, (1, G, 1))
    block_mix = jnp.where((mask_rows == mask_cols)[None], tiled_mix, jnp.zeros_like(tiled_mix))

    def process_group(group_index):
        start_row = group_index * RG
        group_filters = lax.dynamic_slice_in_dim(filters, start_row, RG, 0)
        response_sum = jnp.zeros((RG * K, lon_dev * chans), jnp.float32)
        for block_index in range(NB):
            start_lon = (SMAX * lon_dev + shifts[group_index, block_index]) * chans
            window = lax.dynamic_slice(
                extended, (start_row, start_lon), (tall_rows, (lon_dev + BW) * chans)
            )
            stacked = jnp.concatenate(
                [window[:, column * chans : (column + lon_dev) * chans] for column in range(BW)],
                axis=0,
            )
            weights = group_filters[:, block_index].astype(jnp.float32).reshape(RG, K, span, BW)
            padded = jnp.einsum("pkrt,pra->pkta", weights, placement)
            left_side = padded.reshape(RG * K, BW * tall_rows).astype(jnp.bfloat16)
            response_sum = response_sum + jnp.dot(
                left_side, stacked, preferred_element_type=jnp.float32
            )
        response = response_sum.astype(jnp.bfloat16).reshape(RG, K, lon_dev, chans)
        mixed = jnp.zeros((RG * lon_dev, chans), jnp.float32)
        for basis in range(K):
            mixed = mixed + jnp.dot(
                response[:, basis].reshape(RG * lon_dev, chans),
                block_mix[basis],
                preferred_element_type=jnp.float32,
            )
        return mixed.astype(jnp.bfloat16).reshape(RG, lon_dev, chans)

    results = lax.map(process_group, jnp.arange(groups, dtype=jnp.int32))
    return results.reshape(rows, lon_dev, chans)


def solution(mesh):
    return jax.shard_map(
        on_device,
        mesh=mesh,
        in_specs=(P("lat", "lon", None), P("lat", None, None, None), P("lat"), P("lat", None), P()),
        out_specs=P("lat", "lon", None),
        check_vma=False,
    )
```

profile of v0, /device:TPU:1, one launch (start us, length us, event | category | flops | bytes accessed | tf_op | source)
XLA Modules:
  0.0 310.1 jit_solution(14346610511943409242)
XLA Ops:
  0.0 1.3 copy.30
  1.3 4.5 %collective-permute-start = (bf16[16,16384]{1,0:T(8,128)(2,1)S(1)}, bf16[16,16384]{1,0:T(8,128)(2,1)S(1)}, u32[]{:S(2)}, u32[]{:S(2)}) collective-permute-start(bf16[16,16384]{1,0:T(8,128)(2,1)S(1)} %bitcast.204), channel_id=1, source_target_pairs={{0,8},{8,16},{16,24},{1,9},{9,17},{17,25},{2,10},{10,18},{18,26},{... | collective-permute-start | bytes 1572872 | tf_op jit(solution)/shard_map/ppermute | solution.py:28
  5.9 1.9 collective-permute-start.1
  7.8 4.2 %collective-permute-done = bf16[16,16384]{1,0:T(8,128)(2,1)S(1)} collective-permute-done((bf16[16,16384]{1,0:T(8,128)(2,1)S(1)}, bf16[16,16384]{1,0:T(8,128)(2,1)S(1)}, u32[]{:S(2)}, u32[]{:S(2)}) %collective-permute-start) | collective-permute-done | bytes 524320 | tf_op jit(solution)/shard_map/ppermute | solution.py:28
  12.0 0.9 constant_dynamic-update-slice_fusion.3
  12.9 0.8 constant_dynamic-update-slice_fusion.2
  13.7 3.1 collective-permute-done.1
  16.8 0.9 constant_dynamic-update-slice_fusion.1
  17.6 1.3 collective-permute-start.2
  19.2 1.1 bitcast_select_fusion
  21.6 1.2 collective-permute-start.3
  22.8 3.0 collective-permute-start.4
  26.0 30.2 %collective-permute-done.2 = bf16[48,16384]{1,0:T(8,128)(2,1)} collective-permute-done((bf16[48,16384]{1,0:T(8,128)(2,1)}, bf16[48,16384]{1,0:T(8,128)(2,1)}, u32[]{:S(2)}, u32[]{:S(2)}) %collective-permute-start.2) | collective-permute-done | bytes 1572896 | tf_op jit(solution)/shard_map/ppermute | solution.py:18
  56.2 1.5 constant_dynamic-update-slice_fusion.8
  57.7 32.9 %collective-permute-done.3 = bf16[48,16384]{1,0:T(8,128)(2,1)S(1)} collective-permute-done((bf16[48,16384]{1,0:T(8,128)(2,1)}, bf16[48,16384]{1,0:T(8,128)(2,1)S(1)}, u32[]{:S(2)}, u32[]{:S(2)}) %collective-permute-start.3) | collective-permute-done | bytes 1572896 | tf_op jit(solution)/shard_map/ppermute | solution.py:18
  91.0 25.8 %collective-permute-done.5 = bf16[48,16384]{1,0:T(8,128)(2,1)S(1)} collective-permute-done((bf16[48,16384]{1,0:T(8,128)(2,1)}, bf16[48,16384]{1,0:T(8,128)(2,1)S(1)}, u32[]{:S(2)}, u32[]{:S(2)}) %collective-permute-start.5) | collective-permute-done | bytes 1572896 | tf_op jit(solution)/shard_map/ppermute | solution.py:18
  116.9 3.0 copy-done
  120.0 190.1 %while.12 = (s32[]{:T(128)}, bf16[2,8,64,256]{3,2,1,0:T(8,128)(2,1)}, s32[2]{0:T(128)S(1)}, bf16[16,4,9,264]{3,1,2,0:T(4,128)(2,1)S(1)}, s32[2,4]{1,0:T(2,128)S(...) while((s32[]{:T(128)}, ...), condition=%wide.region_1.2_spmd.clone.clone, body=%wide.region_0.1_spmd.clone.clone.sunk | while | flops 3636078592 | bytes 185017056 | solution.py:91
  124.2 2.5 dynamic-slice_dynamic-update-slice_fusion.41
  128.5 4.9 %dynamic-slice_dynamic-update-slice_fusion.42 = (bf16[320,16384]{1,0:T(8,128)(2,1)}, bf16[320,16384]{1,0:T(8,128)(2,1)}, bf16[320,16384]{1,0:T(8,128)(2,1)}, bf16[320,16384]{1,0:T(8,128)(2,1)}) fusion(bf16[320,16384]{1,0:T(8,128)(2,1)} %dynamic-slice_dynamic-update-slice_fusion.41, bf16[48,81920]{1,0:T(8,128)(2,1)} %get-tuple-element.362, ...), kind=kLoop, calls=%fused_computation.11.clone.1 | loop fusion | bytes 10485780 | tf_op jit(solution)/shard_map/while
  133.4 5.0 %dynamic-slice_dynamic-update-slice_fusion.43 = (bf16[320,16384]{1,0:T(8,128)(2,1)}, bf16[320,16384]{1,0:T(8,128)(2,1)}, bf16[320,16384]{1,0:T(8,128)(2,1)}, bf16[320,16384]{1,0:T(8,128)(2,1)}) fusion(bf16[320,16384]{1,0:T(8,128)(2,1)} %get-tuple-element.262, bf16[48,81920]{1,0:T(8,128)(2,1)} %get-tuple-element.362, s32[]{:T(128)S(6)} %select_n.75, ...), kind=kLoop, calls=%fused_computation.10.clone.1 | loop fusion | bytes 10485780 | tf_op jit(solution)/shard_map/while
  138.4 4.9 %dynamic-slice_dynamic-update-slice_fusion.44 = (bf16[320,16384]{1,0:T(8,128)(2,1)}, bf16[320,16384]{1,0:T(8,128)(2,1)}, bf16[320,16384]{1,0:T(8,128)(2,1)}, bf16[320,16384]{1,0:T(8,128)(2,1)}) fusion(bf16[320,16384]{1,0:T(8,128)(2,1)} %get-tuple-element.266, bf16[48,81920]{1,0:T(8,128)(2,1)} %get-tuple-element.362, s32[]{:T(128)S(6)} %select_n.75, ...), kind=kLoop, calls=%fused_computation.9.clone.1 | loop fusion | bytes 10485780 | tf_op jit(solution)/shard_map/while
  143.3 4.9 %dynamic-slice_dynamic-update-slice_fusion.45 = (bf16[320,16384]{1,0:T(8,128)(2,1)}, bf16[320,16384]{1,0:T(8,128)(2,1)}, bf16[320,16384]{1,0:T(8,128)(2,1)}, bf16[320,16384]{1,0:T(8,128)(2,1)}) fusion(bf16[320,16384]{1,0:T(8,128)(2,1)} %get-tuple-element.270, bf16[48,81920]{1,0:T(8,128)(2,1)} %get-tuple-element.362, s32[]{:T(128)S(6)} %select_n.75, ...), kind=kLoop, calls=%fused_computation.8.clone.1 | loop fusion | bytes 10485780 | tf_op jit(solution)/shard_map/while
  148.3 4.9 %dynamic-slice_dynamic-update-slice_fusion.46 = (bf16[320,16384]{1,0:T(8,128)(2,1)}, bf16[320,16384]{1,0:T(8,128)(2,1)}, bf16[320,16384]{1,0:T(8,128)(2,1)}, bf16[320,16384]{1,0:T(8,128)(2,1)}) fusion(bf16[320,16384]{1,0:T(8,128)(2,1)} %get-tuple-element.274, bf16[48,81920]{1,0:T(8,128)(2,1)} %get-tuple-element.362, s32[]{:T(128)S(6)} %select_n.75, ...), kind=kLoop, calls=%fused_computation.7.clone.1 | loop fusion | bytes 10485780 | tf_op jit(solution)/shard_map/while
  153.2 4.9 %dynamic-slice_dynamic-update-slice_fusion.47 = (bf16[320,16384]{1,0:T(8,128)(2,1)}, bf16[320,16384]{1,0:T(8,128)(2,1)}, bf16[320,16384]{1,0:T(8,128)(2,1)}, bf16[320,16384]{1,0:T(8,128)(2,1)}) fusion(bf16[320,16384]{1,0:T(8,128)(2,1)} %get-tuple-element.278, bf16[48,81920]{1,0:T(8,128)(2,1)} %get-tuple-element.362, s32[]{:T(128)S(6)} %select_n.75, ...), kind=kLoop, calls=%fused_computation.6.clone.1 | loop fusion | bytes 10485780 | tf_op jit(solution)/shard_map/while
  158.1 4.9 %dynamic-slice_dynamic-update-slice_fusion.48 = (bf16[320,16384]{1,0:T(8,128)(2,1)}, bf16[320,16384]{1,0:T(8,128)(2,1)}, bf16[320,16384]{1,0:T(8,128)(2,1)}, bf16[320,16384]{1,0:T(8,128)(2,1)}) fusion(bf16[320,16384]{1,0:T(8,128)(2,1)} %get-tuple-element.282, bf16[48,81920]{1,0:T(8,128)(2,1)} %get-tuple-element.362, s32[]{:T(128)S(6)} %select_n.75, ...), kind=kLoop, calls=%fused_computation.5.clone.1 | loop fusion | bytes 10485780 | tf_op jit(solution)/shard_map/while/body/eval_jaxpr/concatenate | solution.py:71
  163.0 4.1 %dynamic-slice_dynamic-update-slice_fusion.49 = (bf16[320,16384]{1,0:T(8,128)(2,1)}, bf16[320,16384]{1,0:T(8,128)(2,1)}, bf16[320,16384]{1,0:T(8,128)(2,1)}) fusion(bf16[320,16384]{1,0:T(8,128)(2,1)} %get-tuple-element.286, bf16[48,81920]{1,0:T(8,128)(2,1)} %get-tuple-element.362, s32[]{:T(128)S(6)} %select_n.75, s32[]{:T(128)S(6)} %add.319, ...), kind=kLoop, calls=%fused_computation.13.clone.1 | loop fusion | bytes 7864336 | tf_op jit(solution)/shard_map/while/body/eval_jaxpr/concatenate | solution.py:71
  167.1 1.3 dynamic-slice_reduce_fusion.5
  170.0 8.5 %fusion.127 = f32[72,16384]{1,0:T(8,128)} fusion(bf16[72,320]{1,0:T(8,128)(2,1)S(1)} %convert_element_type.114, bf16[320,16384]{1,0:T(8,128)(2,1)} %get-tuple-element.289), kind=kOutput, calls=%fused_computation.107.clone.1 | convolution fusion | flops 754974720 | bytes 15250432 | tf_op jit(solution)/shard_map/while/body/eval_jaxpr/dot_general | solution.py:78
  180.1 9.9 %convolution_add_fusion.20 = f32[72,16384]{1,0:T(8,128)} fusion(f32[72,16384]{1,0:T(8,128)} %fusion.127, bf16[72,320]{1,0:T(8,128)(2,1)S(1)} %convert_element_type.115, bf16[320,16384]{1,0:T(8,128)(2,1)} %get-tuple-element.291), kind=kOutput, calls=%fused_computation.3.clone.1 | convolution fusion | flops 756154368 | bytes 19969024 | tf_op jit(solution)/shard_map/while/body/eval_jaxpr/dot_general | solution.py:78
  191.5 9.9 %convolution_add_fusion.21 = f32[72,16384]{1,0:T(8,128)} fusion(f32[72,16384]{1,0:T(8,128)} %convolution_add_fusion.20, bf16[72,320]{1,0:T(8,128)(2,1)S(1)} %convert_element_type.116, bf16[320,16384]{1,0:T(8,128)(2,1)} %get-tuple-element.293), kind=kOutput, calls=%fused_computation.2.clone.1 | convolution fusion | flops 756154368 | bytes 19969024 | tf_op jit(solution)/shard_map/while/body/eval_jaxpr/dot_general | solution.py:78
  203.0 7.8 %fusion.128 = bf16[72,16384]{1,0:T(8,128)(2,1)S(1)} fusion(f32[72,16384]{1,0:T(8,128)} %convolution_add_fusion.21, bf16[72,320]{1,0:T(8,128)(2,1)S(1)} %convert_element_type.117, bf16[320,16384]{1,0:T(8,128)(2,1)} %get-tuple-element.295), kind=kOutput, calls=%fused_computation.4.clone.1 | convolution fusion | flops 757334016 | bytes 17609728 | tf_op jit(solution)/shard_map/while/body/eval_jaxpr/dot_general | solution.py:78
  213.8 0.8 copy-done.5
  218.8 2.5 dynamic-slice_dynamic-update-slice_fusion.41
  223.1 5.0 %dynamic-slice_dynamic-update-slice_fusion.42 = (bf16[320,16384]{1,0:T(8,128)(2,1)}, bf16[320,16384]{1,0:T(8,128)(2,1)}, bf16[320,16384]{1,0:T(8,128)(2,1)}, bf16[320,16384]{1,0:T(8,128)(2,1)}) fusion(bf16[320,16384]{1,0:T(8,128)(2,1)} %dynamic-slice_dynamic-update-slice_fusion.41, bf16[48,81920]{1,0:T(8,128)(2,1)} %get-tuple-element.362, ...), kind=kLoop, calls=%fused_computation.11.clone.1 | loop fusion | bytes 10485780 | tf_op jit(solution)/shard_map/while
  228.2 5.1 %dynamic-slice_dynamic-update-slice_fusion.43 = (bf16[320,16384]{1,0:T(8,128)(2,1)}, bf16[320,16384]{1,0:T(8,128)(2,1)}, bf16[320,16384]{1,0:T(8,128)(2,1)}, bf16[320,16384]{1,0:T(8,128)(2,1)}) fusion(bf16[320,16384]{1,0:T(8,128)(2,1)} %get-tuple-element.262, bf16[48,81920]{1,0:T(8,128)(2,1)} %get-tuple-element.362, s32[]{:T(128)S(6)} %select_n.75, ...), kind=kLoop, calls=%fused_computation.10.clone.1 | loop fusion | bytes 10485780 | tf_op jit(solution)/shard_map/while
  233.3 5.1 %dynamic-slice_dynamic-update-slice_fusion.44 = (bf16[320,16384]{1,0:T(8,128)(2,1)}, bf16[320,16384]{1,0:T(8,128)(2,1)}, bf16[320,16384]{1,0:T(8,128)(2,1)}, bf16[320,16384]{1,0:T(8,128)(2,1)}) fusion(bf16[320,16384]{1,0:T(8,128)(2,1)} %get-tuple-element.266, bf16[48,81920]{1,0:T(8,128)(2,1)} %get-tuple-element.362, s32[]{:T(128)S(6)} %select_n.75, ...), kind=kLoop, calls=%fused_computation.9.clone.1 | loop fusion | bytes 10485780 | tf_op jit(solution)/shard_map/while
  238.4 5.1 %dynamic-slice_dynamic-update-slice_fusion.45 = (bf16[320,16384]{1,0:T(8,128)(2,1)}, bf16[320,16384]{1,0:T(8,128)(2,1)}, bf16[320,16384]{1,0:T(8,128)(2,1)}, bf16[320,16384]{1,0:T(8,128)(2,1)}) fusion(bf16[320,16384]{1,0:T(8,128)(2,1)} %get-tuple-element.270, bf16[48,81920]{1,0:T(8,128)(2,1)} %get-tuple-element.362, s32[]{:T(128)S(6)} %select_n.75, ...), kind=kLoop, calls=%fused_computation.8.clone.1 | loop fusion | bytes 10485780 | tf_op jit(solution)/shard_map/while
  243.5 5.0 %dynamic-slice_dynamic-update-slice_fusion.46 = (bf16[320,16384]{1,0:T(8,128)(2,1)}, bf16[320,16384]{1,0:T(8,128)(2,1)}, bf16[320,16384]{1,0:T(8,128)(2,1)}, bf16[320,16384]{1,0:T(8,128)(2,1)}) fusion(bf16[320,16384]{1,0:T(8,128)(2,1)} %get-tuple-element.274, bf16[48,81920]{1,0:T(8,128)(2,1)} %get-tuple-element.362, s32[]{:T(128)S(6)} %select_n.75, ...), kind=kLoop, calls=%fused_computation.7.clone.1 | loop fusion | bytes 10485780 | tf_op jit(solution)/shard_map/while
  248.5 5.1 %dynamic-slice_dynamic-update-slice_fusion.47 = (bf16[320,16384]{1,0:T(8,128)(2,1)}, bf16[320,16384]{1,0:T(8,128)(2,1)}, bf16[320,16384]{1,0:T(8,128)(2,1)}, bf16[320,16384]{1,0:T(8,128)(2,1)}) fusion(bf16[320,16384]{1,0:T(8,128)(2,1)} %get-tuple-element.278, bf16[48,81920]{1,0:T(8,128)(2,1)} %get-tuple-element.362, s32[]{:T(128)S(6)} %select_n.75, ...), kind=kLoop, calls=%fused_computation.6.clone.1 | loop fusion | bytes 10485780 | tf_op jit(solution)/shard_map/while
  253.5 5.0 %dynamic-slice_dynamic-update-slice_fusion.48 = (bf16[320,16384]{1,0:T(8,128)(2,1)}, bf16[320,16384]{1,0:T(8,128)(2,1)}, bf16[320,16384]{1,0:T(8,128)(2,1)}, bf16[320,16384]{1,0:T(8,128)(2,1)}) fusion(bf16[320,16384]{1,0:T(8,128)(2,1)} %get-tuple-element.282, bf16[48,81920]{1,0:T(8,128)(2,1)} %get-tuple-element.362, s32[]{:T(128)S(6)} %select_n.75, ...), kind=kLoop, calls=%fused_computation.5.clone.1 | loop fusion | bytes 10485780 | tf_op jit(solution)/shard_map/while/body/eval_jaxpr/concatenate | solution.py:71
  258.5 4.1 %dynamic-slice_dynamic-update-slice_fusion.49 = (bf16[320,16384]{1,0:T(8,128)(2,1)}, bf16[320,16384]{1,0:T(8,128)(2,1)}, bf16[320,16384]{1,0:T(8,128)(2,1)}) fusion(bf16[320,16384]{1,0:T(8,128)(2,1)} %get-tuple-element.286, bf16[48,81920]{1,0:T(8,128)(2,1)} %get-tuple-element.362, s32[]{:T(128)S(6)} %select_n.75, s32[]{:T(128)S(6)} %add.319, ...), kind=kLoop, calls=%fused_computation.13.clone.1 | loop fusion | bytes 7864336 | tf_op jit(solution)/shard_map/while/body/eval_jaxpr/concatenate | solution.py:71
  262.6 1.3 dynamic-slice_reduce_fusion.5
  265.5 8.5 %fusion.127 = f32[72,16384]{1,0:T(8,128)} fusion(bf16[72,320]{1,0:T(8,128)(2,1)S(1)} %convert_element_type.114, bf16[320,16384]{1,0:T(8,128)(2,1)} %get-tuple-element.289), kind=kOutput, calls=%fused_computation.107.clone.1 | convolution fusion | flops 754974720 | bytes 15250432 | tf_op jit(solution)/shard_map/while/body/eval_jaxpr/dot_general | solution.py:78
  275.6 9.9 %convolution_add_fusion.20 = f32[72,16384]{1,0:T(8,128)} fusion(f32[72,16384]{1,0:T(8,128)} %fusion.127, bf16[72,320]{1,0:T(8,128)(2,1)S(1)} %convert_element_type.115, bf16[320,16384]{1,0:T(8,128)(2,1)} %get-tuple-element.291), kind=kOutput, calls=%fused_computation.3.clone.1 | convolution fusion | flops 756154368 | bytes 19969024 | tf_op jit(solution)/shard_map/while/body/eval_jaxpr/dot_general | solution.py:78
  287.0 9.9 %convolution_add_fusion.21 = f32[72,16384]{1,0:T(8,128)} fusion(f32[72,16384]{1,0:T(8,128)} %convolution_add_fusion.20, bf16[72,320]{1,0:T(8,128)(2,1)S(1)} %convert_element_type.116, bf16[320,16384]{1,0:T(8,128)(2,1)} %get-tuple-element.293), kind=kOutput, calls=%fused_computation.2.clone.1 | convolution fusion | flops 756154368 | bytes 19969024 | tf_op jit(solution)/shard_map/while/body/eval_jaxpr/dot_general | solution.py:78
  298.4 7.8 %fusion.128 = bf16[72,16384]{1,0:T(8,128)(2,1)S(1)} fusion(f32[72,16384]{1,0:T(8,128)} %convolution_add_fusion.21, bf16[72,320]{1,0:T(8,128)(2,1)S(1)} %convert_element_type.117, bf16[320,16384]{1,0:T(8,128)(2,1)} %get-tuple-element.295), kind=kOutput, calls=%fused_computation.4.clone.1 | convolution fusion | flops 757334016 | bytes 17609728 | tf_op jit(solution)/shard_map/while/body/eval_jaxpr/dot_general | solution.py:78
  309.3 0.8 copy-done.5
  (96 shorter events, 23.0 us)
Async XLA Ops:
  1.3 10.6 %collective-permute-start = (bf16[16,16384]{1,0:T(8,128)(2,1)S(1)}, bf16[16,16384]{1,0:T(8,128)(2,1)S(1)}, u32[]{:S(2)}, u32[]{:S(2)}) collective-permute-start(bf16[16,16384]{1,0:T(8,128)(2,1)S(1)} %bitcast.204), channel_id=1, source_target_pairs={{0,8},{8,16},{16,24},{1,9},{9,17},{17,25},{2,10},{10,18},{18,26},{... | collective-permute-start | bytes 1572872 | tf_op jit(solution)/shard_map/ppermute | solution.py:28
  5.9 10.9 %collective-permute-start.1 = (bf16[16,16384]{1,0:T(8,128)(2,1)S(1)}, bf16[16,16384]{1,0:T(8,128)(2,1)S(1)}, u32[]{:S(2)}, u32[]{:S(2)}) collective-permute-start(bf16[16,16384]{1,0:T(8,128)(2,1)S(1)} %bitcast.205), channel_id=1, source_target_pairs={{8,0},{16,8},{24,16},{9,1},{17,9},{25,17},{10,2},{18,10},{26,18},{... | collective-permute-start | bytes 1572872 | tf_op jit(solution)/shard_map/ppermute | solution.py:29
  12.0 7.0 %copy-start.2 = (bf16[16,16384]{1,0:T(8,128)(2,1)}, bf16[16,16384]{1,0:T(8,128)(2,1)S(1)}, u32[]{:S(2)}) copy-start(bf16[16,16384]{1,0:T(8,128)(2,1)S(1)} %collective-permute-done) | copy-start | bytes 1572868
  17.6 38.6 %collective-permute-start.2 = (bf16[48,16384]{1,0:T(8,128)(2,1)}, bf16[48,16384]{1,0:T(8,128)(2,1)}, u32[]{:S(2)}, u32[]{:S(2)}) collective-permute-start(bf16[48,16384]{1,0:T(8,128)(2,1)} %constant_dynamic-update-slice_fusion.1), channel_id=1, source_target_pairs={{0,2},{1,3},{2,4},{3,5},{4,6},{5,7},{6,0},{7,1},{8,10},{9,11},{10,... | collective-permute-start | bytes 4718600 | tf_op jit(solution)/shard_map/ppermute | solution.py:18
  19.1 71.6 %copy-start.3 = (bf16[16,16384]{1,0:T(8,128)(2,1)S(1)}, bf16[16,16384]{1,0:T(8,128)(2,1)}, u32[]{:S(2)}) copy-start(bf16[16,16384]{1,0:T(8,128)(2,1)} %copy-done.2) | copy-start | bytes 1572868
  21.6 98.4 %copy-start.1 = (bf16[16,4,9,264]{3,1,2,0:T(4,128)(2,1)S(1)}, bf16[16,4,9,264]{3,1,2,0:T(4,128)(2,1)}, u32[]{:S(2)}) copy-start(bf16[16,4,9,264]{3,1,2,0:T(4,128)(2,1)} %param.8) | copy-start | bytes 912388
  21.6 69.0 %collective-permute-start.3 = (bf16[48,16384]{1,0:T(8,128)(2,1)}, bf16[48,16384]{1,0:T(8,128)(2,1)S(1)}, u32[]{:S(2)}, u32[]{:S(2)}) collective-permute-start(bf16[48,16384]{1,0:T(8,128)(2,1)} %constant_dynamic-update-slice_fusion.1), channel_id=1, source_target_pairs={{0,1},{1,2},{2,3},{3,4},{4,5},{5,6},{6,7},{7,0},{8,9},{9,10},{10,1... | collective-permute-start | bytes 4718600 | tf_op jit(solution)/shard_map/ppermute | solution.py:18
  22.8 68.0 %collective-permute-start.4 = (bf16[48,16384]{1,0:T(8,128)(2,1)}, bf16[48,16384]{1,0:T(8,128)(2,1)S(1)}, u32[]{:S(2)}, u32[]{:S(2)}) collective-permute-start(bf16[48,16384]{1,0:T(8,128)(2,1)} %constant_dynamic-update-slice_fusion.1), channel_id=1, source_target_pairs={{0,7},{1,0},{2,1},{3,2},{4,3},{5,4},{6,5},{7,6},{8,15},{9,8},{10,9... | collective-permute-start | bytes 4718600 | tf_op jit(solution)/shard_map/ppermute | solution.py:18
  25.8 91.0 %collective-permute-start.5 = (bf16[48,16384]{1,0:T(8,128)(2,1)}, bf16[48,16384]{1,0:T(8,128)(2,1)S(1)}, u32[]{:S(2)}, u32[]{:S(2)}) collective-permute-start(bf16[48,16384]{1,0:T(8,128)(2,1)} %constant_dynamic-update-slice_fusion.1), channel_id=1, source_target_pairs={{0,6},{1,7},{2,0},{3,1},{4,2},{5,3},{6,4},{7,5},{8,14},{9,15},{10,... | collective-permute-start | bytes 4718600 | tf_op jit(solution)/shard_map/ppermute | solution.py:18
  116.9 3.1 copy-start
  211.4 2.4 copy-start.4
  213.8 0.8 copy-start.5
  306.8 2.4 copy-start.4
  309.3 0.8 copy-start.5
where the time goes:
time: 311 us; the launch traced here: 310 us
  local copies, waits for them, and re-layouts  111 us (36%)
  waiting for transfers between devices  96.1 us (31%)
  matrix products  78 us (25%)
  starting transfers between devices  12.2 us (4%)
  loops' own time  10.1 us (3%)
    ppermute x4, waiting for transfers between devices, from_behind(): return lax.ppermute(value, axis, pairs)  88.9 us
    dot_general x8, matrix products, process_group(): jnp.dot(left_side, stacked, preferred_element_type=jnp.float32)  72.2 us
    while x24, local copies, waits for them, and re-layouts  67.7 us
    concatenate x4, local copies, waits for them, and re-layouts, process_group(): jnp.concatenate([window[:, column * chans:(column + lon_dev) * chans] for...  18 us
    another operation x1, loops' own time, on_device(): results = lax.map(process_group, jnp.arange(groups, dtype=jnp.int32))  10.1 us
    reshape x16, local copies, waits for them, and re-layouts, process_group(): group_filters[:, block_index].astype(jnp.float32).reshape(RG, K, span, BW)  9 us
    unnamed x17, local copies, waits for them, and re-layouts  7.92 us
  transfers between devices with their start and end apart: 6, of which 5 were waited for; matrix products, arithmetic and copies ran while one was open for 2% of the time, Pallas kernels for 0%

commit v1 on v0

v1 whole, which is shorter than its diff:
```python
import jax
import jax.numpy as jnp
from jax import lax
from jax.experimental import pallas as pl
from jax.experimental.pallas import tpu as pltpu
from jax.sharding import PartitionSpec as P

K = 9
G = 8
R = 16
RG = 8
NB = 4
BW = 8
SMAX = 2
CG = 32
LANES = 128
WIDE = G * CG
PER = LANES // CG
TALL = RG + 2 * R
SLAB = TALL * BW
VMEM_LIMIT = 56 * 1024 * 1024


def swap_chunks(parts):
    rows = parts[0].shape[0]
    chunk = lax.broadcasted_iota(jnp.int32, (rows, LANES), 1) // CG
    outs = []
    for g in range(G):
        g1, g0 = divmod(g, PER)
        halves = []
        for m1 in range(G // PER):
            acc = None
            for m0 in range(PER):
                piece = parts[m1 * PER + m0][:, g1 * LANES : (g1 + 1) * LANES]
                turn = (CG * (m0 - g0)) % LANES
                if turn:
                    piece = pltpu.roll(piece, turn, 1)
                acc = piece if acc is None else jnp.where(chunk == m0, piece, acc)
            halves.append(acc)
        outs.append(jnp.concatenate(halves, axis=1))
    return outs


def pack_kernel(field_ref, out_ref):
    rows = field_ref.shape[0]
    value = field_ref[...].astype(jnp.float32).reshape(rows, G, BW, WIDE)
    parts = [value[:, m].reshape(rows * BW, WIDE) for m in range(G)]
    for g, block in enumerate(swap_chunks(parts)):
        out_ref[g] = block.astype(jnp.bfloat16)


def unpack_kernel(in_ref, out_ref):
    rows = out_ref.shape[0]
    parts = [in_ref[g].astype(jnp.float32) for g in range(G)]
    blocks = [b.reshape(rows, 1, BW, WIDE) for b in swap_chunks(parts)]
    whole = jnp.concatenate(blocks, axis=1).reshape(rows, G * BW, WIDE)
    out_ref[...] = whole.astype(jnp.bfloat16)


def toeplitz_kernel(spread_ref, out_ref):
    groups = spread_ref.shape[0]
    width = 2 * SLAB
    v = lax.broadcasted_iota(jnp.int32, (BW, width), 0)
    lane = lax.broadcasted_iota(jnp.int32, (BW, width), 1)
    u = lane % BW
    score = jnp.where(lane < SLAB, u - v, v - u - 1)
    keep = score >= 0
    keep_first = jnp.where(lane // BW == TALL - 1, -1, score) >= 0
    keep_last = jnp.where(lane // BW == TALL, -1, score) >= 0

    def body(index, carry):
        group, k = index // K, index % K
        rows = spread_ref[group, k]
        blocks = []
        for p in range(RG):
            kept = {0: keep_first, RG - 1: keep_last}.get(p, keep)
            pieces = []
            for b in range(NB):
                row = rows[p : p + 1, b * width : (b + 1) * width]
                wide = jnp.broadcast_to(row, (BW, width))
                turned = pltpu.roll(wide, 0, 1, stride=1, stride_axis=0)
                pieces.append(jnp.where(kept, turned, 0.0))
            blocks.append(jnp.concatenate(pieces, axis=1))
        tall = jnp.concatenate(blocks, axis=0).astype(jnp.bfloat16)
        out_ref[group, pl.ds(pl.multiple_of(k * RG * BW, RG * BW), RG * BW), :] = tall
        return carry

    lax.fori_loop(0, groups * K, body, 0)


def main_kernel(shift_ref, ext_ref, weights_ref, mix_ref, out_ref, turned, side, response):
    sectors = ext_ref.shape[0]
    rows = ext_ref.shape[1]
    groups = weights_ref.shape[0]
    lane = lax.broadcasted_iota(jnp.int32, (rows, LANES), 1)

    def turn(sector, carry):
        after = jnp.minimum(sector + 1, sectors - 1)
        first = ext_ref[sector][:, :LANES].astype(jnp.float32)
        second = ext_ref[sector][:, LANES:].astype(jnp.float32)
        third = ext_ref[after][:, :LANES].astype(jnp.float32)
        turned[0, 2 * sector] = ext_ref[sector][:, :LANES]
        turned[0, 2 * sector + 1] = ext_ref[sector][:, LANES:]
        for r in range(1, PER):
            back = LANES - CG * r
            x, y, z = [pltpu.roll(t, back, 1) for t in (first, second, third)]
            turned[r, 2 * sector] = jnp.where(lane < back, x, y).astype(jnp.bfloat16)
            turned[r, 2 * sector + 1] = jnp.where(lane < back, y, z).astype(jnp.bfloat16)
        return carry

    lax.fori_loop(0, sectors, turn, 0)

    for group in range(groups):

        def tile(s, carry):
            for b in range(NB):
                for half in range(2):
                    shift = shift_ref[group, b] + (half + SMAX * BW)
                    r, step = shift % PER, shift // PER
                    low = (b * 2 + half) * SLAB
                    for j in range(2):
                        side[low : low + SLAB, j * LANES : (j + 1) * LANES] = turned[
                            r, 2 * s + j + step, group * RG * BW : group * RG * BW + SLAB, :
                        ]
            sums = jnp.dot(weights_ref[group], side[...], preferred_element_type=jnp.float32)
            rounded = sums.astype(jnp.bfloat16)
            for k in range(K):
                response[k, s] = rounded[k * RG * BW : (k + 1) * RG * BW]
            return carry

        lax.fori_loop(0, G, tile, 0)
        mixed = jnp.zeros((G * RG * BW, WIDE), jnp.float32)
        for k in range(K):
            left = response[k].reshape(G * RG * BW, WIDE)
            mixed = mixed + jnp.dot(left, mix_ref[k], preferred_element_type=jnp.float32)
        out_ref[:, group * RG * BW : (group + 1) * RG * BW, :] = mixed.astype(jnp.bfloat16).reshape(
            G, RG * BW, WIDE
        )


def spread_filters(filters):
    rows = filters.shape[0]
    groups = rows // RG
    taps = filters.shape[3]
    f = filters.reshape(groups, RG, NB, K, taps).transpose(0, 3, 1, 2, 4)
    placed = []
    for p in range(RG):
        one = f[:, :, p]
        low = jnp.pad(one, ((0, 0), (0, 0), (0, 0), (BW * p, 2 * SLAB - BW * p - taps)))
        start = SLAB - BW + BW * p
        high = jnp.pad(one, ((0, 0), (0, 0), (0, 0), (start, 2 * SLAB - start - taps)))
        placed.append(low + high)
    whole = jnp.stack(placed, axis=2)
    return whole.reshape(groups, K, RG, NB * 2 * SLAB).astype(jnp.float32)


def call(kernel, shape, *args, scratch=(), specs=None):
    return pl.pallas_call(
        kernel,
        out_shape=jax.ShapeDtypeStruct(shape, jnp.bfloat16),
        in_specs=specs or [pl.BlockSpec(memory_space=pltpu.VMEM)] * len(args),
        out_specs=pl.BlockSpec(memory_space=pltpu.VMEM),
        scratch_shapes=list(scratch),
        compiler_params=pltpu.CompilerParams(vmem_limit_bytes=VMEM_LIMIT),
    )(*args)


def on_device(field, filters, sector_width, block_offset, mixing):
    rows, lon_dev, chans = field.shape
    groups = rows // RG
    lons = lax.axis_size("lon")
    lats = lax.axis_size("lat")
    segments = lons // G
    cuts = None
    if segments > 1:
        cuts = [[s * G + i for i in range(G)] for s in range(segments)]
    channel_group = lax.axis_index("lon") % G

    packed = call(pack_kernel, (G, rows * BW, WIDE), field)
    own = lax.all_to_all(packed, "lon", 0, 0, axis_index_groups=cuts, tiled=True)
    up = [(i, i + 1) for i in range(lats - 1)]
    down = [(i + 1, i) for i in range(lats - 1)]
    above = lax.ppermute(own, "lat", up)
    below = lax.ppermute(own, "lat", down)
    tall = jnp.concatenate([above, own, below], axis=1)
    if segments > 1:
        forward = [(i, (i + G) % lons) for i in range(lons)]
        back = [(j, i) for i, j in forward]
        west = lax.ppermute(tall[G - SMAX :], "lon", forward)
        east = lax.ppermute(tall[:SMAX], "lon", back)
    else:
        west, east = tall[G - SMAX :], tall[:SMAX]
    ext = jnp.concatenate([west, tall, east], axis=0)

    weights = call(toeplitz_kernel, (groups, K * RG * BW, NB * 2 * SLAB), spread_filters(filters))
    own_mix = lax.dynamic_slice_in_dim(mixing, channel_group * CG, CG, 2)
    eye = (jnp.arange(WIDE)[:, None] // CG) == (jnp.arange(WIDE)[None, :] // CG)
    big_mix = jnp.where(eye[None], jnp.tile(own_mix, (1, G, G)), jnp.zeros((), mixing.dtype))
    shifts = block_offset * sector_width[:, None]

    vmem = pl.BlockSpec(memory_space=pltpu.VMEM)
    mixed = call(
        main_kernel,
        (G, rows * BW, WIDE),
        shifts,
        ext,
        weights,
        big_mix,
        scratch=[
            pltpu.VMEM((PER, 2 * (G + 2 * SMAX), (rows + 2 * R) * BW, LANES), jnp.bfloat16),
            pltpu.VMEM((NB * 2 * SLAB, WIDE), jnp.bfloat16),
            pltpu.VMEM((K, G, RG * BW, WIDE), jnp.bfloat16),
        ],
        specs=[pl.BlockSpec(memory_space=pltpu.SMEM), vmem, vmem, vmem],
    )
    home = lax.all_to_all(mixed, "lon", 0, 0, axis_index_groups=cuts, tiled=True)
    return call(unpack_kernel, (rows, lon_dev, chans), home)


def solution(mesh):
    return jax.shard_map(
        on_device,
        mesh=mesh,
        in_specs=(P("lat", "lon", None), P("lat", None, None, None), P("lat"), P("lat", None), P()),
        out_specs=P("lat", "lon", None),
        check_vma=False,
    )
```

time: 311 us -> 104 us (0.33)
  local copies, waits for them, and re-layouts: 111 us -> 13.4 us
  matrix products: 78 us -> 0 us
  waiting for transfers between devices: 96.1 us -> 18.7 us
  Pallas kernels: 0 us -> 38.2 us
  blocking collectives: 0 us -> 13.3 us
  loops' own time: 10.1 us -> 0 us
  other arithmetic: 2.65 us -> 5.79 us
    ppermute x6 -> x2, waiting for transfers between devices: 96.1 us -> 7.28 us  [the longest x1 7.28 us: on_device(): below = lax.ppermute(own, 'lat', down)]
    dot_general x34 -> x0, matrix products: 78 us -> none  [the longest x8 72.2 us: process_group(): jnp.dot(left_side, stacked, preferred_element_type=jnp.float32)]
    while x24 -> x0, local copies, waits for them, and re-layouts: 67.7 us -> none
    pallas_call x0 -> x4, Pallas kernels: none -> 38.2 us  [call(): pl.pallas_call(kernel, out_shape=jax.ShapeDtypeStruct(shape, jnp.bfloat16...]
    concatenate x6 -> x1, local copies, waits for them, and re-layouts: 19 us -> 0.03 us  [on_device(): tall = jnp.concatenate([above, own, below], axis=1)]
    all_to_all x0 -> x1, blocking collectives: none -> 13.3 us  [on_device(): lax.all_to_all(mixed, 'lon', 0, 0, axis_index_groups=cuts, tiled=True)]
    another operation x0 -> x19, local copies, waits for them, and re-layouts: none -> 12.9 us  [the longest x2 9.11 us: on_device(): jnp.tile(own_mix, (1, G, G))]
    all_to_all x0 -> x1, waiting for transfers between devices: none -> 11.4 us  [on_device(): lax.all_to_all(packed, 'lon', 0, 0, axis_index_groups=cuts, tiled=True)]
  transfers between devices with their start and end apart: 6 -> 3, of which waited for: 5 -> 2; matrix products, arithmetic and copies ran while one was open for 2% -> 17% of each run, Pallas kernels for 0% -> 7%
where the time goes in v1:
time: 104 us; the launch traced here: 103 us
  Pallas kernels  38.2 us (37%)
  waiting for transfers between devices  18.7 us (18%)
  local copies, waits for them, and re-layouts  13.4 us (13%)
  starting transfers between devices  13.3 us (13%)
  blocking collectives  13.3 us (13%)
  other arithmetic  5.79 us (6%)
    pallas_call x4, Pallas kernels, call(): pl.pallas_call(kernel, out_shape=jax.ShapeDtypeStruct(shape, jnp.bfloat16...  38.2 us
    all_to_all x1, blocking collectives, on_device(): lax.all_to_all(mixed, 'lon', 0, 0, axis_index_groups=cuts, tiled=True)  13.3 us
    all_to_all x1, waiting for transfers between devices, on_device(): lax.all_to_all(packed, 'lon', 0, 0, axis_index_groups=cuts, tiled=True)  11.4 us
    another operation x2, local copies, waits for them, and re-layouts, on_device(): jnp.tile(own_mix, (1, G, G))  9.11 us
    ppermute x1, waiting for transfers between devices, on_device(): below = lax.ppermute(own, 'lat', down)  7.28 us
    all_to_all x1, starting transfers between devices, on_device(): lax.all_to_all(packed, 'lon', 0, 0, axis_index_groups=cuts, tiled=True)  6.35 us
    ppermute x1, starting transfers between devices, on_device(): above = lax.ppermute(own, 'lat', up)  5.04 us
    another operation x17, local copies, waits for them, and re-layouts, spread_filters(): whole = jnp.stack(placed, axis=2)  3.76 us
  transfers between devices with their start and end apart: 3, of which 2 were waited for; matrix products, arithmetic and copies ran while one was open for 17% of the time, Pallas kernels for 7%

profile of v1, /device:TPU:1, one launch (start us, length us, event | category | flops | bytes accessed | tf_op | source)
XLA Modules:
  0.0 103.1 jit_solution(15007388059931014525)
XLA Ops:
  0.0 0.0 copy-start
  0.0 0.0 copy-start.1
  0.0 2.4 %shard_map.55 = bf16[8,128,256]{2,1,0:T(8,128)(2,1)} custom-call(bf16[16,64,256]{2,1,0:T(8,128)(2,1)} %field_ref.1), custom_call_target="tpu_custom_call" | custom-call | tf_op jit(solution)/shard_map/pallas_call | solution.py:158
  2.4 6.4 %all-to-all-start = ((bf16[8,128,256]{2,1,0:T(8,128)(2,1)}), bf16[8,128,256]{2,1,0:T(8,128)(2,1)S(1)}, u32[]{:S(2)}, u32[]{:S(2)}) async-start(bf16[8,128,256]{2,1,0:T(8,128)(2,1)} %shard_map.55), calls=%async_computation | async-start | bytes 1048576 | tf_op jit(solution)/shard_map/all_to_all | solution.py:180
  8.8 0.0 copy-start.2
  8.8 0.0 copy-start.3
  8.8 0.0 copy-done.1
  8.8 0.2 copy.17
  9.0 0.0 copy-done
  9.0 0.1 constant_dynamic-slice_fusion
  9.1 0.2 slice_bitcast_fusion
  9.2 0.2 pad_add_fusion.4
  9.5 0.2 pad_add_fusion.2
  9.7 0.2 pad_add_fusion
  9.9 0.2 pad_add_fusion.6
  10.1 0.0 copy-done.2
  10.1 0.0 copy-done.3
  10.1 0.7 broadcast_multiply_fusion.shift_ref
  10.7 11.4 %all-to-all-done = bf16[8,128,256]{2,1,0:T(8,128)(2,1)S(1)} async-done(((bf16[8,128,256]{2,1,0:T(8,128)(2,1)}), bf16[8,128,256]{2,1,0:T(8,128)(2,1)S(1)}, u32[]{:S(2)}, u32[]{:S(2)}) %all-to-all-start) | async-done | bytes 524320 | tf_op jit(solution)/shard_map/all_to_all | solution.py:180
  22.2 5.0 %collective-permute-start = (bf16[8,128,256]{2,1,0:T(8,128)(2,1)S(1)}, bf16[8,128,256]{2,1,0:T(8,128)(2,1)S(1)}, u32[]{:S(2)}, u32[]{:S(2)}) collective-permute-start(bf16[8,128,256]{2,1,0:T(8,128)(2,1)S(1)} %all-to-all-done), channel_id=1, source_target_pairs={{0,8},{8,16},{16,24},{1,9},{9,17},{17,25},{2,10},{10,18},{18,26},{... | collective-permute-start | bytes 1572872 | tf_op jit(solution)/shard_map/ppermute | solution.py:183
  27.3 0.1 copy.10
  27.5 0.1 copy.11
  27.7 0.1 copy.12
  27.9 0.1 copy.13
  28.1 0.1 copy.14
  28.3 0.1 copy.15
  28.5 0.1 copy.8
  28.7 0.1 copy.9
  28.8 2.3 %stack.35 = bf16[2,9,8,2560]{3,2,1,0:T(8,128)(2,1)S(1)} concatenate(bf16[2,9,1,2560]{3,2,1,0:T(2,128)(2,1)S(1)} %copy.8, bf16[2,9,1,2560]{3,2,1,0:T(2,128)(2,1)S(1)} %copy.9, bf16[2,9,1,2560]{3,2,1,0:T(2,128)(2,1)S(1)} %copy.10, bf16[2,9,1,2560]{3,2,1,0:T(2,128)(2,1)S(1)} %copy.11, bf16[2,9,1,2560]{3,2,1,0:T(2,128)(2,1)S(1)} %copy.12, bf16[2,9,1,2560]{3,2,1,0:T(2,128)(2,1)S(1)} %copy.13, ...), dimensions={2} | concatenate | bytes 1474560 | tf_op jit(solution)/shard_map/stack | solution.py:153
  31.1 1.3 %convert_element_type.35.spread_ref = f32[2,9,8,2560]{3,2,1,0:T(8,128)} convert(bf16[2,9,8,2560]{3,2,1,0:T(8,128)(2,1)S(1)} %stack.35) | non-fusion elementwise | flops 368640 | bytes 2211840 | tf_op jit(solution)/shard_map/convert_element_type | solution.py:154
  32.4 6.9 %shard_map.56.weights_ref = bf16[2,576,2560]{2,1,0:T(8,128)(2,1)} custom-call(f32[2,9,8,2560]{3,2,1,0:T(8,128)} %convert_element_type.35.spread_ref), custom_call_target="tpu_custom_call" | custom-call | tf_op jit(solution)/shard_map/pallas_call | solution.py:158
  39.3 3.3 %tile.4 = bf16[9,8,32,8,32]{4,3,2,1,0:T(8,128)(2,1)} broadcast(bf16[9,32,32]{2,1,0:T(8,128)(2,1)S(1)} %constant_dynamic-slice_fusion), dimensions={0,2,4} | broadcast | bytes 1198080 | tf_op jit(solution)/shard_map/tile | solution.py:198
  42.6 5.8 %tile.10 = bf16[9,256,256]{2,1,0:T(8,128)(2,1)S(1)} reshape(bf16[9,8,32,8,32]{4,3,2,1,0:T(8,128)(2,1)} %tile.4) | data formatting | bytes 2359296 | tf_op jit(solution)/shard_map/tile | solution.py:198
  48.4 0.1 broadcast_compare_fusion
  48.5 1.9 %collective-permute-start.1 = (bf16[8,128,256]{2,1,0:T(8,128)(2,1)S(1)}, bf16[8,128,256]{2,1,0:T(8,128)(2,1)S(1)}, u32[]{:S(2)}, u32[]{:S(2)}) collective-permute-start(bf16[8,128,256]{2,1,0:T(8,128)(2,1)S(1)} %all-to-all-done), channel_id=1, source_target_pairs={{8,0},{16,8},{24,16},{9,1},{17,9},{25,17},{10,2},{18,10},{26,18},{... | collective-permute-start | bytes 1572872 | tf_op jit(solution)/shard_map/ppermute | solution.py:184
  50.4 1.2 %broadcast_select_fusion.mix_ref = bf16[9,256,256]{2,1,0:T(8,128)(2,1)} fusion(bf16[9,256,256]{2,1,0:T(8,128)(2,1)S(1)} %tile.10, pred[256,256]{1,0:T(8,128)(4,1)S(1)} %broadcast_compare_fusion), kind=kLoop, calls=%fused_computation.1 | loop fusion | flops 589824 | bytes 2424832 | tf_op jit(solution)/shard_map/jit(_where)/select_n | solution.py:198
  51.6 0.0 collective-permute-done
  51.7 7.3 %collective-permute-done.1 = bf16[8,128,256]{2,1,0:T(8,128)(2,1)S(1)} collective-permute-done((bf16[8,128,256]{2,1,0:T(8,128)(2,1)S(1)}, bf16[8,128,256]{2,1,0:T(8,128)(2,1)S(1)}, u32[]{:S(2)}, u32[]{:S(2)}) %collective-permute-start.1) | collective-permute-done | bytes 524320 | tf_op jit(solution)/shard_map/ppermute | solution.py:184
  59.0 0.1 fusion
  59.1 1.7 %pad_maximum_fusion.ext_ref = bf16[12,384,256]{2,1,0:T(8,128)(2,1)} fusion(bf16[2,384,256]{2,1,0:T(8,128)(2,1)S(1)} %get-tuple-element.6, bf16[8,384,256]{2,1,0:T(8,128)(2,1)S(1)} %constant_dynamic-update-slice_fusion, bf16[2,384,256]{2,1,0:T(8,128)(2,1)S(1)} %get-tuple-element.5), kind=kLoop, calls=%fused_computation | loop fusion | flops 2359296 | bytes 4718592 | tf_op jit(solution)/shard_map/concatenate | solution.py:193
  60.8 26.6 %shard_map.57 = bf16[8,128,256]{2,1,0:T(8,128)(2,1)} custom-call(s32[2,4]{1,0:T(2,128)} %broadcast_multiply_fusion.shift_ref, bf16[12,384,256]{2,1,0:T(8,128)(2,1)} %pad_maximum_fusion.ext_ref, bf16[2,576,2560]{2,1,0:T(8,128)(2,1)} %shard_map.56.weights_ref, bf16[9,256,256]{2,1,0:T(8,128)(2,1)} %broadcast_select_fusion.mix_ref), custom_call_target="tpu_custom_call" | custom-call | tf_op jit(solution)/shard_map/pallas_call | solution.py:158
  87.4 13.3 %all_to_all.10.in_ref = bf16[8,128,256]{2,1,0:T(8,128)(2,1)} all-to-all(bf16[8,128,256]{2,1,0:T(8,128)(2,1)} %shard_map.57), channel_id=1, replica_groups=mesh['lat'=4,'lon'=8] {'lon'}, dimensions={0} | all-to-all | bytes 1048576 | tf_op jit(solution)/shard_map/all_to_all | solution.py:216
  100.8 2.3 %shard_map.58 = bf16[16,64,256]{2,1,0:T(8,128)(2,1)} custom-call(bf16[8,128,256]{2,1,0:T(8,128)(2,1)} %all_to_all.10.in_ref), custom_call_target="tpu_custom_call" | custom-call | tf_op jit(solution)/shard_map/pallas_call | solution.py:158
  (12 shorter events, 0.4 us)
Async XLA Ops:
  0.0 9.0 %copy-start = (bf16[9,32,256]{2,1,0:T(8,128)(2,1)S(1)}, bf16[9,32,256]{2,1,0:T(8,128)(2,1)}, u32[]{:S(2)}) copy-start(bf16[9,32,256]{2,1,0:T(8,128)(2,1)} %param.9) | copy-start | bytes 442372
  0.0 8.8 %copy-start.1 = (bf16[16,4,9,264]{3,1,2,0:T(4,128)(2,1)S(1)}, bf16[16,4,9,264]{3,1,2,0:T(4,128)(2,1)}, u32[]{:S(2)}) copy-start(bf16[16,4,9,264]{3,1,2,0:T(4,128)(2,1)} %param.6) | copy-start | bytes 912388
  2.4 19.8 %all-to-all-start = ((bf16[8,128,256]{2,1,0:T(8,128)(2,1)}), bf16[8,128,256]{2,1,0:T(8,128)(2,1)S(1)}, u32[]{:S(2)}, u32[]{:S(2)}) async-start(bf16[8,128,256]{2,1,0:T(8,128)(2,1)} %shard_map.55), calls=%async_computation | async-start | bytes 1048576 | tf_op jit(solution)/shard_map/all_to_all | solution.py:180
  8.8 1.3 %copy-start.2 = (s32[2,4]{1,0:T(2,128)S(1)}, s32[2,4]{1,0:T(2,128)}, u32[]{:S(2)}) copy-start(s32[2,4]{1,0:T(2,128)} %param.8) | copy-start | bytes 100
  8.8 1.3 %copy-start.3 = (s32[2]{0:T(128)S(1)}, s32[2]{0:T(128)}, u32[]{:S(2)}) copy-start(s32[2]{0:T(128)} %param.7) | copy-start | bytes 28
  22.2 29.5 %collective-permute-start = (bf16[8,128,256]{2,1,0:T(8,128)(2,1)S(1)}, bf16[8,128,256]{2,1,0:T(8,128)(2,1)S(1)}, u32[]{:S(2)}, u32[]{:S(2)}) collective-permute-start(bf16[8,128,256]{2,1,0:T(8,128)(2,1)S(1)} %all-to-all-done), channel_id=1, source_target_pairs={{0,8},{8,16},{16,24},{1,9},{9,17},{17,25},{2,10},{10,18},{18,26},{... | collective-permute-start | bytes 1572872 | tf_op jit(solution)/shard_map/ppermute | solution.py:183
  48.5 10.5 %collective-permute-start.1 = (bf16[8,128,256]{2,1,0:T(8,128)(2,1)S(1)}, bf16[8,128,256]{2,1,0:T(8,128)(2,1)S(1)}, u32[]{:S(2)}, u32[]{:S(2)}) collective-permute-start(bf16[8,128,256]{2,1,0:T(8,128)(2,1)S(1)} %all-to-all-done), channel_id=1, source_target_pairs={{8,0},{16,8},{24,16},{9,1},{17,9},{25,17},{10,2},{18,10},{26,18},{... | collective-permute-start | bytes 1572872 | tf_op jit(solution)/shard_map/ppermute | solution.py:184

commit v2 on v1

v2 whole, which is shorter than its diff:
```python
import functools

import jax
import jax.numpy as jnp
from jax import lax
from jax.experimental import pallas as pl
from jax.experimental.pallas import tpu as pltpu
from jax.sharding import PartitionSpec as P

K = 9
G = 8
R = 16
RG = 8
NB = 4
BW = 8
SMAX = 2
CG = 32
LANES = 128
WIDE = G * CG
PER = LANES // CG
TALL = RG + 2 * R
SLAB = TALL * BW
VMEM_LIMIT = 56 * 1024 * 1024


def swap_chunks(parts):
    rows = parts[0].shape[0]
    chunk = lax.broadcasted_iota(jnp.int32, (rows, LANES), 1) // CG
    outs = []
    for g in range(G):
        g1, g0 = divmod(g, PER)
        halves = []
        for m1 in range(G // PER):
            acc = None
            for m0 in range(PER):
                piece = parts[m1 * PER + m0][:, g1 * LANES : (g1 + 1) * LANES]
                turn = (CG * (m0 - g0)) % LANES
                if turn:
                    piece = pltpu.roll(piece, turn, 1)
                acc = piece if acc is None else jnp.where(chunk == m0, piece, acc)
            halves.append(acc)
        outs.append(jnp.concatenate(halves, axis=1))
    return outs


def peers(steps):
    me = lax.axis_index("lon") % G
    base = lax.axis_index("lon") - me
    other = (me + steps) % G
    return other, (lax.axis_index("lat"), base + other)


def lay_filters(spread_ref, out_ref, first, last):
    width = 2 * SLAB
    v = lax.broadcasted_iota(jnp.int32, (BW, width), 0)
    lane = lax.broadcasted_iota(jnp.int32, (BW, width), 1)
    u = lane % BW
    keep_low = jnp.where(lane < SLAB, u - v, -1) >= 0
    keep_high = jnp.where(lane < SLAB, -1, v - u - 1) >= 0

    def body(index, carry):
        group, k = index // K, index % K
        rows = spread_ref[group, k]
        blocks = []
        for p in range(RG):
            pieces = []
            for b in range(NB):
                row = rows[p : p + 1, b * width : (b + 1) * width]
                wide = jnp.broadcast_to(row, (BW, width))
                low = pltpu.roll(wide, BW * p, 1, stride=1, stride_axis=0)
                high = pltpu.roll(wide, SLAB - BW + BW * p, 1, stride=1, stride_axis=0)
                pieces.append(jnp.where(keep_low, low, jnp.where(keep_high, high, 0.0)))
            blocks.append(jnp.concatenate(pieces, axis=1))
        tall = jnp.concatenate(blocks, axis=0).astype(jnp.bfloat16)
        out_ref[group, pl.ds(pl.multiple_of(k * RG * BW, RG * BW), RG * BW), :] = tall
        return carry

    lax.fori_loop(first, last, body, 0)


def exchange_kernel(lats, field_ref, spread_ref, tall_ref, weights_ref, packed, sent, got, halo_sent, halo_got):
    rows = field_ref.shape[0]
    size = rows * BW
    lat, lon = lax.axis_index("lat"), lax.axis_index("lon")
    me, _ = peers(0)
    has_up, has_down = lat > 0, lat < lats - 1
    barrier = pltpu.get_barrier_semaphore()
    for d in range(1, G):
        pl.semaphore_signal(barrier, inc=1, device_id=peers(d)[1], device_id_type=pl.DeviceIdType.MESH)

    @pl.when(has_up)
    def _():
        pl.semaphore_signal(barrier, inc=1, device_id=(lat - 1, lon), device_id_type=pl.DeviceIdType.MESH)

    @pl.when(has_down)
    def _():
        pl.semaphore_signal(barrier, inc=1, device_id=(lat + 1, lon), device_id_type=pl.DeviceIdType.MESH)

    value = field_ref[...].astype(jnp.float32).reshape(rows, G, BW, WIDE)
    parts = [value[:, m].reshape(size, WIDE) for m in range(G)]
    for g, block in enumerate(swap_chunks(parts)):
        packed[g] = block.astype(jnp.bfloat16)

    count = G - 1 + jnp.where(has_up, 1, 0) + jnp.where(has_down, 1, 0)
    pl.semaphore_wait(barrier, count)

    def swap(d):
        other, device = peers(d)
        return pltpu.make_async_remote_copy(
            src_ref=packed.at[other],
            dst_ref=tall_ref.at[me, pl.ds(size, size)],
            send_sem=sent.at[d],
            recv_sem=got.at[d],
            device_id=device,
            device_id_type=pl.DeviceIdType.MESH,
        )

    def halo(d, side):
        sector, _ = peers(G - d)
        return pltpu.make_async_remote_copy(
            src_ref=tall_ref.at[sector, pl.ds(size, size)],
            dst_ref=tall_ref.at[sector, pl.ds(0 if side else 2 * size, size)],
            send_sem=halo_sent.at[side, d],
            recv_sem=halo_got.at[side, d],
            device_id=(lat + 1 if side else lat - 1, lon),
            device_id_type=pl.DeviceIdType.MESH,
        )

    order = [1, 7, 2, 6, 3, 5, 4]
    for d in order:
        swap(d).start()
    tall_ref[me, size : 2 * size] = packed[me]

    def forward(d):
        @pl.when(has_up)
        def _():
            halo(d, 0).start()

        @pl.when(has_down)
        def _():
            halo(d, 1).start()

    forward(0)
    steps = spread_ref.shape[0] * K
    lay_filters(spread_ref, weights_ref, 0, steps // 2)
    for d in order:
        swap(d).wait_recv()
        forward(d)
    lay_filters(spread_ref, weights_ref, steps // 2, steps)

    blank = jnp.zeros((G, size, WIDE), jnp.bfloat16)

    @pl.when(lat == 0)
    def _():
        tall_ref[:, 0:size] = blank

    @pl.when(lat == lats - 1)
    def _():
        tall_ref[:, 2 * size : 3 * size] = blank

    for d in order:
        swap(d).wait_send()
    for d in range(G):

        @pl.when(has_up)
        def _():
            halo(d, 0).wait_send()
            halo(d, 1).wait_recv()

        @pl.when(has_down)
        def _():
            halo(d, 1).wait_send()
            halo(d, 0).wait_recv()


def home_kernel(in_ref, out_ref, held, sent, got):
    rows = out_ref.shape[0]
    me, _ = peers(0)
    barrier = pltpu.get_barrier_semaphore()
    for d in range(1, G):
        pl.semaphore_signal(barrier, inc=1, device_id=peers(d)[1], device_id_type=pl.DeviceIdType.MESH)
    pl.semaphore_wait(barrier, G - 1)

    def swap(d):
        other, device = peers(d)
        return pltpu.make_async_remote_copy(
            src_ref=in_ref.at[other],
            dst_ref=held.at[me],
            send_sem=sent.at[d],
            recv_sem=got.at[d],
            device_id=device,
            device_id_type=pl.DeviceIdType.MESH,
        )

    for d in range(1, G):
        swap(d).start()
    held[me] = in_ref[me]
    for d in range(1, G):
        swap(d).wait_recv()
    parts = [held[g].astype(jnp.float32) for g in range(G)]
    blocks = [b.reshape(rows, 1, BW, WIDE) for b in swap_chunks(parts)]
    whole = jnp.concatenate(blocks, axis=1).reshape(rows, G * BW, WIDE)
    out_ref[...] = whole.astype(jnp.bfloat16)
    for d in range(1, G):
        swap(d).wait_send()


def make_mix(group, mixing_ref, big):
    lane = lax.broadcasted_iota(jnp.int32, (CG, WIDE), 1) // CG
    row_block = lax.broadcasted_iota(jnp.int32, (WIDE, WIDE), 0) // CG
    lane_block = lax.broadcasted_iota(jnp.int32, (WIDE, WIDE), 1) // CG
    for k in range(K):
        one = jnp.where(lane == group, mixing_ref[k].astype(jnp.float32), 0.0)
        for turn in (CG, 2 * CG, 4 * CG):
            one = one + pltpu.roll(one, turn, 1)
        tall = jnp.concatenate([one] * G, axis=0)
        big[k] = jnp.where(row_block == lane_block, tall, 0.0).astype(jnp.bfloat16)


def main_kernel(shift_ref, ext_ref, weights_ref, mixing_ref, out_ref, turned, side, response, mix_ref):
    sectors = ext_ref.shape[0]
    rows = ext_ref.shape[1]
    groups = weights_ref.shape[0]
    lane = lax.broadcasted_iota(jnp.int32, (rows, LANES), 1)
    make_mix(shift_ref[0, NB], mixing_ref, mix_ref)

    def turn(sector, carry):
        after = jnp.minimum(sector + 1, sectors - 1)
        first = ext_ref[sector][:, :LANES].astype(jnp.float32)
        second = ext_ref[sector][:, LANES:].astype(jnp.float32)
        third = ext_ref[after][:, :LANES].astype(jnp.float32)
        turned[0, 2 * sector] = ext_ref[sector][:, :LANES]
        turned[0, 2 * sector + 1] = ext_ref[sector][:, LANES:]
        for r in range(1, PER):
            back = LANES - CG * r
            x, y, z = [pltpu.roll(t, back, 1) for t in (first, second, third)]
            turned[r, 2 * sector] = jnp.where(lane < back, x, y).astype(jnp.bfloat16)
            turned[r, 2 * sector + 1] = jnp.where(lane < back, y, z).astype(jnp.bfloat16)
        return carry

    lax.fori_loop(0, sectors, turn, 0)

    for group in range(groups):

        def tile(s, carry):
            for b in range(NB):
                for half in range(2):
                    shift = shift_ref[group, b] + (half + SMAX * BW)
                    r, step = shift % PER, shift // PER
                    low = (b * 2 + half) * SLAB
                    for j in range(2):
                        side[low : low + SLAB, j * LANES : (j + 1) * LANES] = turned[
                            r, 2 * s + j + step, group * RG * BW : group * RG * BW + SLAB, :
                        ]
            sums = jnp.dot(weights_ref[group], side[...], preferred_element_type=jnp.float32)
            rounded = sums.astype(jnp.bfloat16)
            for k in range(K):
                response[k, s] = rounded[k * RG * BW : (k + 1) * RG * BW]
            return carry

        lax.fori_loop(0, G, tile, 0)
        mixed = jnp.zeros((G * RG * BW, WIDE), jnp.float32)
        for k in range(K):
            left = response[k].reshape(G * RG * BW, WIDE)
            mixed = mixed + jnp.dot(left, mix_ref[k], preferred_element_type=jnp.float32)
        out_ref[:, group * RG * BW : (group + 1) * RG * BW, :] = mixed.astype(jnp.bfloat16).reshape(
            G, RG * BW, WIDE
        )


def spread_filters(filters):
    rows = filters.shape[0]
    groups = rows // RG
    taps = filters.shape[3]
    f = filters.reshape(groups, RG, NB, K, taps).transpose(0, 3, 1, 2, 4)
    f = jnp.pad(f.astype(jnp.float32), ((0, 0),) * 4 + ((0, 2 * SLAB - taps),))
    return f.reshape(groups, K, RG, NB * 2 * SLAB)


def call(kernel, shapes, *args, scratch=(), specs=None, ident=None):
    vmem = pl.BlockSpec(memory_space=pltpu.VMEM)
    return pl.pallas_call(
        kernel,
        out_shape=[jax.ShapeDtypeStruct(shape, jnp.bfloat16) for shape in shapes],
        in_specs=specs or [vmem] * len(args),
        out_specs=[vmem] * len(shapes),
        scratch_shapes=list(scratch),
        compiler_params=pltpu.CompilerParams(
            vmem_limit_bytes=VMEM_LIMIT, collective_id=ident, has_side_effects=ident is not None
        ),
    )(*args)


def on_device(field, filters, sector_width, block_offset, mixing):
    rows, lon_dev, chans = field.shape
    groups = rows // RG
    lons = lax.axis_size("lon")
    lats = lax.axis_size("lat")
    segments = lons // G
    size = rows * BW
    copies = pltpu.SemaphoreType.DMA((G,))
    halos = pltpu.SemaphoreType.DMA((2, G))

    tall, weights = call(
        functools.partial(exchange_kernel, lats),
        [(G, 3 * size, WIDE), (groups, K * RG * BW, NB * 2 * SLAB)],
        field,
        spread_filters(filters),
        scratch=[pltpu.VMEM((G, size, WIDE), jnp.bfloat16), copies, copies, halos, halos],
        ident=0,
    )
    if segments > 1:
        forward = [(i, (i + G) % lons) for i in range(lons)]
        back = [(j, i) for i, j in forward]
        west = lax.ppermute(tall[G - SMAX :], "lon", forward)
        east = lax.ppermute(tall[:SMAX], "lon", back)
    else:
        west, east = tall[G - SMAX :], tall[:SMAX]
    ext = jnp.concatenate([west, tall, east], axis=0)

    shifts = block_offset * sector_width[:, None]
    channel_group = jnp.broadcast_to(lax.axis_index("lon") % G, (groups, 1))
    scalars = jnp.concatenate([shifts, channel_group.astype(jnp.int32)], axis=1)

    vmem = pl.BlockSpec(memory_space=pltpu.VMEM)
    (mixed,) = call(
        main_kernel,
        [(G, size, WIDE)],
        scalars,
        ext,
        weights,
        mixing,
        scratch=[
            pltpu.VMEM((PER, 2 * (G + 2 * SMAX), (rows + 2 * R) * BW, LANES), jnp.bfloat16),
            pltpu.VMEM((NB * 2 * SLAB, WIDE), jnp.bfloat16),
            pltpu.VMEM((K, G, RG * BW, WIDE), jnp.bfloat16),
            pltpu.VMEM((K, WIDE, WIDE), jnp.bfloat16),
        ],
        specs=[pl.BlockSpec(memory_space=pltpu.SMEM), vmem, vmem, vmem],
    )
    (out,) = call(
        home_kernel,
        [(rows, lon_dev, chans)],
        mixed,
        scratch=[pltpu.VMEM((G, size, WIDE), jnp.bfloat16), copies, copies],
        ident=1,
    )
    return out


def solution(mesh):
    return jax.shard_map(
        on_device,
        mesh=mesh,
        in_specs=(P("lat", "lon", None), P("lat", None, None, None), P("lat"), P("lat", None), P()),
        out_specs=P("lat", "lon", None),
        check_vma=False,
    )
```

time: 104 us -> 77.4 us (0.74)
  Pallas kernels: 38.2 us -> 67.2 us
  waiting for transfers between devices: 18.7 us -> 0 us
  blocking collectives: 13.3 us -> 0 us
  starting transfers between devices: 13.3 us -> 0 us
  local copies, waits for them, and re-layouts: 13.4 us -> 5.19 us
  other arithmetic: 5.79 us -> 3.81 us
    pallas_call x4 -> x3, Pallas kernels: 38.2 us -> 67.2 us  [call(): pl.pallas_call(kernel, out_shape=[jax.ShapeDtypeStruct(shape, jnp.bfloat1...]
    all_to_all x1 -> x0, blocking collectives: 13.3 us -> none  [on_device(): lax.all_to_all(mixed, 'lon', 0, 0, axis_index_groups=cuts, tiled=True)]
    another operation x19 -> x0, local copies, waits for them, and re-layouts: 12.9 us -> none  [the longest x2 9.11 us: on_device(): jnp.tile(own_mix, (1, G, G))]
    all_to_all x1 -> x0, waiting for transfers between devices: 11.4 us -> none  [on_device(): lax.all_to_all(packed, 'lon', 0, 0, axis_index_groups=cuts, tiled=True)]
    ppermute x2 -> x0, waiting for transfers between devices: 7.28 us -> none  [the longest x1 7.28 us: on_device(): below = lax.ppermute(own, 'lat', down)]
    ppermute x2 -> x0, starting transfers between devices: 6.96 us -> none  [the longest x1 5.04 us: on_device(): above = lax.ppermute(own, 'lat', up)]
    all_to_all x1 -> x0, starting transfers between devices: 6.35 us -> none  [on_device(): lax.all_to_all(packed, 'lon', 0, 0, axis_index_groups=cuts, tiled=True)]
    unnamed x10 -> x3, local copies, waits for them, and re-layouts: 0.09 us -> 2.23 us
  transfers between devices with their start and end apart: 3 -> 0, of which waited for: 2 -> 0; matrix products, arithmetic and copies ran while one was open for 17% -> 0% of each run, Pallas kernels for 7% -> 0%
where the time goes in v2:
time: 77.4 us; the launch traced here: 76.2 us
  Pallas kernels  67.2 us (87%)
  local copies, waits for them, and re-layouts  5.19 us (7%)
  other arithmetic  3.81 us (5%)
    pallas_call x3, Pallas kernels, call(): pl.pallas_call(kernel, out_shape=[jax.ShapeDtypeStruct(shape, jnp.bfloat1...  67.2 us
    unnamed x3, local copies, waits for them, and re-layouts  2.23 us
    concatenate x1, other arithmetic, on_device(): ext = jnp.concatenate([west, tall, east], axis=0)  1.69 us

profile of v2, /device:TPU:1, one launch (start us, length us, event | category | flops | bytes accessed | tf_op | source)
XLA Modules:
  0.0 76.2 jit_solution(8609362798158775821)
XLA Ops:
  0.0 0.8 broadcast_multiply_fusion
  0.8 0.5 concatenate.6.shift_ref
  1.3 1.1 %copy.8 = bf16[2,8,4,9,264]{4,1,2,3,0:T(8,128)(2,1)S(1)} copy(bf16[2,8,4,9,264]{4,2,3,1,0:T(4,128)(2,1)} %bitcast.8) | data formatting | bytes 608256 | tf_op jit(solution)/shard_map/convert_element_type | solution.py:276
  2.4 0.1 pad.6
  2.4 1.4 %convert.5.spread_ref = f32[2,9,8,2560]{3,2,1,0:T(8,128)} convert(bf16[2,9,8,2560]{3,2,1,0:T(8,128)(2,1)S(1)} %bitcast.6) | non-fusion elementwise | flops 368640 | bytes 2211840 | tf_op jit(solution)/shard_map/reshape | solution.py:277
  3.8 26.3 %shard_map.55 = (bf16[8,384,256]{2,1,0:T(8,128)(2,1)}, bf16[2,576,2560]{2,1,0:T(8,128)(2,1)}) custom-call(bf16[16,64,256]{2,1,0:T(8,128)(2,1)} %field_ref.1, f32[2,9,8,2560]{3,2,1,0:T(8,128)} %convert.5.spread_ref), custom_call_target="tpu_custom_call" | custom-call | tf_op jit(solution)/shard_map/pallas_call | solution.py:282
  30.1 0.0 copy-start
  30.1 1.3 %fusion = (bf16[2,384,256]{2,1,0:T(8,128)(2,1)S(1)}, bf16[2,384,256]{2,1,0:T(8,128)(2,1)S(1)}) fusion(bf16[8,384,256]{2,1,0:T(8,128)(2,1)} %get-tuple-element.7), kind=kLoop, calls=%fused_computation.3 | loop fusion | bytes 1572864 | tf_op jit(solution)/shard_map/slice | solution.py:318
  31.4 0.3 copy-done
  31.7 1.7 %pad_maximum_fusion.ext_ref = bf16[12,384,256]{2,1,0:T(8,128)(2,1)} fusion(bf16[2,384,256]{2,1,0:T(8,128)(2,1)S(1)} %get-tuple-element.10, bf16[8,384,256]{2,1,0:T(8,128)(2,1)S(1)} %copy-done, bf16[2,384,256]{2,1,0:T(8,128)(2,1)S(1)} %get-tuple-element.9), kind=kLoop, calls=%fused_computation | loop fusion | flops 2359296 | bytes 4718592 | tf_op jit(solution)/shard_map/concatenate | solution.py:319
  33.4 26.7 %shard_map.56.in_ref = bf16[8,128,256]{2,1,0:T(8,128)(2,1)} custom-call(s32[2,5]{1,0:T(2,128)} %concatenate.6.shift_ref, bf16[12,384,256]{2,1,0:T(8,128)(2,1)} %pad_maximum_fusion.ext_ref, bf16[2,576,2560]{2,1,0:T(8,128)(2,1)} %get-tuple-element.8.weights_ref, bf16[9,32,256]{2,1,0:T(8,128)(2,1)} %mixing_ref.1), custom_call_target="tpu_custom_call" | custom-call | tf_op jit(solution)/shard_map/pallas_call | solution.py:282
  60.1 14.2 %shard_map.57 = bf16[16,64,256]{2,1,0:T(8,128)(2,1)} custom-call(bf16[8,128,256]{2,1,0:T(8,128)(2,1)} %shard_map.56.in_ref), custom_call_target="tpu_custom_call" | custom-call | tf_op jit(solution)/shard_map/pallas_call | solution.py:282
  74.3 1.9 %copy.10 = bf16[16,64,256]{2,1,0:T(8,128)(2,1)} copy(bf16[16,64,256]{2,1,0:T(8,128)(2,1)} %shard_map.57) | data formatting | bytes 1048576
Async XLA Ops:
  30.1 1.6 %copy-start = (bf16[8,384,256]{2,1,0:T(8,128)(2,1)S(1)}, bf16[8,384,256]{2,1,0:T(8,128)(2,1)}, u32[]{:S(2)}) copy-start(bf16[8,384,256]{2,1,0:T(8,128)(2,1)} %get-tuple-element.7) | copy-start | bytes 4718596

commit v3 on v2

--- a/solution.py
+++ b/solution.py
@@ -173,36 +173,12 @@
             halo(d, 0).wait_recv()
 
 
-def home_kernel(in_ref, out_ref, held, sent, got):
+def unpack_kernel(in_ref, out_ref):
     rows = out_ref.shape[0]
-    me, _ = peers(0)
-    barrier = pltpu.get_barrier_semaphore()
-    for d in range(1, G):
-        pl.semaphore_signal(barrier, inc=1, device_id=peers(d)[1], device_id_type=pl.DeviceIdType.MESH)
-    pl.semaphore_wait(barrier, G - 1)
-
-    def swap(d):
-        other, device = peers(d)
-        return pltpu.make_async_remote_copy(
-            src_ref=in_ref.at[other],
-            dst_ref=held.at[me],
-            send_sem=sent.at[d],
-            recv_sem=got.at[d],
-            device_id=device,
-            device_id_type=pl.DeviceIdType.MESH,
-        )
-
-    for d in range(1, G):
-        swap(d).start()
-    held[me] = in_ref[me]
-    for d in range(1, G):
-        swap(d).wait_recv()
-    parts = [held[g].astype(jnp.float32) for g in range(G)]
+    parts = [in_ref[g].astype(jnp.float32) for g in range(G)]
     blocks = [b.reshape(rows, 1, BW, WIDE) for b in swap_chunks(parts)]
     whole = jnp.concatenate(blocks, axis=1).reshape(rows, G * BW, WIDE)
     out_ref[...] = whole.astype(jnp.bfloat16)
-    for d in range(1, G):
-        swap(d).wait_send()
 
 
 def make_mix(group, mixing_ref, big):
@@ -217,15 +193,23 @@
         big[k] = jnp.where(row_block == lane_block, tall, 0.0).astype(jnp.bfloat16)
 
 
-def main_kernel(shift_ref, ext_ref, weights_ref, mixing_ref, out_ref, turned, side, response, mix_ref):
-    sectors = ext_ref.shape[0]
-    rows = ext_ref.shape[1]
+def main_kernel(
+    shift_ref, ext_ref, weights_ref, mixing_ref, out_ref, turned, side, response, mix_ref, mixed_ref, sent, got
+):
+    sectors, rows, _ = ext_ref.shape
     groups = weights_ref.shape[0]
+    tiles = 2 * sectors
+    closed = sectors == G
+    size = RG * BW
+    me, _ = peers(0)
+    barrier = pltpu.get_barrier_semaphore()
+    for d in range(1, G):
+        pl.semaphore_signal(barrier, inc=1, device_id=peers(d)[1], device_id_type=pl.DeviceIdType.MESH)
     lane = lax.broadcasted_iota(jnp.int32, (rows, LANES), 1)
     make_mix(shift_ref[0, NB], mixing_ref, mix_ref)
 
     def turn(sector, carry):
-        after = jnp.minimum(sector + 1, sectors - 1)
+        after = (sector + 1) % sectors
         first = ext_ref[sector][:, :LANES].astype(jnp.float32)
         second = ext_ref[sector][:, LANES:].astype(jnp.float32)
         third = ext_ref[after][:, :LANES].astype(jnp.float32)
@@ -240,32 +224,64 @@
 
     lax.fori_loop(0, sectors, turn, 0)
 
+    def swap(group, d):
+        other, device = peers(d)
+        part = pl.ds(group * size, size)
+        return pltpu.make_async_remote_copy(
+            src_ref=mixed_ref.at[other, part],
+            dst_ref=out_ref.at[me, part],
+            send_sem=sent.at[group, d],
+            recv_sem=got.at[group, d],
+            device_id=device,
+            device_id_type=pl.DeviceIdType.MESH,
+        )
+
     for group in range(groups):
 
-        def tile(s, carry):
+        def fill(slot, s):
             for b in range(NB):
                 for half in range(2):
                     shift = shift_ref[group, b] + (half + SMAX * BW)
                     r, step = shift % PER, shift // PER
                     low = (b * 2 + half) * SLAB
                     for j in range(2):
-                        side[low : low + SLAB, j * LANES : (j + 1) * LANES] = turned[
-                            r, 2 * s + j + step, group * RG * BW : group * RG * BW + SLAB, :
+                        index = 2 * s + j + step
+                        if closed:
+                            index = (index + tiles - 2 * SMAX) % tiles
+                        side[slot, low : low + SLAB, j * LANES : (j + 1) * LANES] = turned[
+                            r, index, group * size : group * size + SLAB, :
                         ]
-            sums = jnp.dot(weights_ref[group], side[...], preferred_element_type=jnp.float32)
+
+        def multiply(slot, s):
+            sums = jnp.dot(weights_ref[group], side[slot], preferred_element_type=jnp.float32)
             rounded = sums.astype(jnp.bfloat16)
             for k in range(K):
-                response[k, s] = rounded[k * RG * BW : (k + 1) * RG * BW]
+                response[k, s] = rounded[k * size : (k + 1) * size]
+
+        def pair(i, carry):
+            fill(1, 2 * i + 1)
+            multiply(0, 2 * i)
+            fill(0, jnp.minimum(2 * i + 2, G - 1))
+            multiply(1, 2 * i + 1)
             return carry
 
-        lax.fori_loop(0, G, tile, 0)
-        mixed = jnp.zeros((G * RG * BW, WIDE), jnp.float32)
+        fill(0, 0)
+        lax.fori_loop(0, G // 2, pair, 0)
+        mixed = jnp.zeros((G * size, WIDE), jnp.float32)
         for k in range(K):
-            left = response[k].reshape(G * RG * BW, WIDE)
+            left = response[k].reshape(G * size, WIDE)
             mixed = mixed + jnp.dot(left, mix_ref[k], preferred_element_type=jnp.float32)
-        out_ref[:, group * RG * BW : (group + 1) * RG * BW, :] = mixed.astype(jnp.bfloat16).reshape(
-            G, RG * BW, WIDE
-        )
+        part = slice(group * size, (group + 1) * size)
+        mixed_ref[:, part, :] = mixed.astype(jnp.bfloat16).reshape(G, size, WIDE)
+        if group == 0:
+            pl.semaphore_wait(barrier, G - 1)
+        for d in range(1, G):
+            swap(group, d).start()
+        out_ref[me, part, :] = mixed_ref[me, part, :]
+
+    for group in range(groups):
+        for d in range(1, G):
+            swap(group, d).wait()
 
 
 def spread_filters(filters):
@@ -314,9 +330,9 @@
         back = [(j, i) for i, j in forward]
         west = lax.ppermute(tall[G - SMAX :], "lon", forward)
         east = lax.ppermute(tall[:SMAX], "lon", back)
+        ext = jnp.concatenate([west, tall, east], axis=0)
     else:
-        west, east = tall[G - SMAX :], tall[:SMAX]
-    ext = jnp.concatenate([west, tall, east], axis=0)
+        ext = tall
 
     shifts = block_offset * sector_width[:, None]
     channel_group = jnp.broadcast_to(lax.axis_index("lon") % G, (groups, 1))
@@ -331,20 +347,18 @@
         weights,
         mixing,
         scratch=[
-            pltpu.VMEM((PER, 2 * (G + 2 * SMAX), (rows + 2 * R) * BW, LANES), jnp.bfloat16),
-            pltpu.VMEM((NB * 2 * SLAB, WIDE), jnp.bfloat16),
+            pltpu.VMEM((PER, 2 * ext.shape[0], (rows + 2 * R) * BW, LANES), jnp.bfloat16),
+            pltpu.VMEM((2, NB * 2 * SLAB, WIDE), jnp.bfloat16),
             pltpu.VMEM((K, G, RG * BW, WIDE), jnp.bfloat16),
             pltpu.VMEM((K, WIDE, WIDE), jnp.bfloat16),
+            pltpu.VMEM((G, size, WIDE), jnp.bfloat16),
+            pltpu.SemaphoreType.DMA((groups, G)),
+            pltpu.SemaphoreType.DMA((groups, G)),
         ],
         specs=[pl.BlockSpec(memory_space=pltpu.SMEM), vmem, vmem, vmem],
-    )
-    (out,) = call(
-        home_kernel,
-        [(rows, lon_dev, chans)],
-        mixed,
-        scratch=[pltpu.VMEM((G, size, WIDE), jnp.bfloat16), copies, copies],
         ident=1,
     )
+    (out,) = call(unpack_kernel, [(rows, lon_dev, chans)], mixed)
     return out
 
 

time: 77.4 us -> 61.6 us (0.80); the launches traced: 76.2 us -> 61.4 us
  Pallas kernels: 67.2 us -> 57.5 us
  local copies, waits for them, and re-layouts: 5.19 us -> 1.7 us
  other arithmetic: 3.81 us -> 2.11 us
    pallas_call x3, Pallas kernels: 67.2 us -> 57.5 us  [call(): pl.pallas_call(kernel, out_shape=[jax.ShapeDtypeStruct(shape, jnp.bfloat1...]
    unnamed x3 -> x0, local copies, waits for them, and re-layouts: 2.23 us -> none
    concatenate x1 -> x0, other arithmetic: 1.69 us -> none  [on_device(): ext = jnp.concatenate([west, tall, east], axis=0)]
    slice x1 -> x0, local copies, waits for them, and re-layouts: 1.29 us -> none  [on_device(): west, east = (tall[G - SMAX:], tall[:SMAX])]
where the time goes in v3:
time: 61.6 us; the launch traced here: 61.4 us
  Pallas kernels  57.5 us (93%)
  other arithmetic  2.11 us (3%)
  local copies, waits for them, and re-layouts  1.7 us (3%)
    pallas_call x3, Pallas kernels, call(): pl.pallas_call(kernel, out_shape=[jax.ShapeDtypeStruct(shape, jnp.bfloat1...  57.5 us
    reshape x1, other arithmetic, spread_filters(): return f.reshape(groups, K, RG, NB * 2 * SLAB)  1.36 us

profile of v3, /device:TPU:1, one launch (start us, length us, event | category | flops | bytes accessed | tf_op | source)
XLA Modules:
  0.0 61.4 jit_solution(15444942565191191377)
XLA Ops:
  0.0 0.8 %broadcast_multiply_fusion = s32[2,4]{1,0:T(2,128)S(1)} fusion(s32[2,4]{1,0:T(2,128)} %param.8, s32[2]{0:T(128)} %param.7), kind=kLoop, calls=%fused_computation.1 | loop fusion | flops 8 | bytes 72 | tf_op jit(solution)/shard_map/mul | solution.py:337
  0.8 0.6 concatenate.3.shift_ref
  1.3 1.1 %copy.8 = bf16[2,8,4,9,264]{4,1,2,3,0:T(8,128)(2,1)S(1)} copy(bf16[2,8,4,9,264]{4,2,3,1,0:T(4,128)(2,1)} %bitcast.8) | data formatting | bytes 608256 | tf_op jit(solution)/shard_map/convert_element_type | solution.py:292
  2.4 0.1 pad.6
  2.5 1.4 %convert.5.spread_ref = f32[2,9,8,2560]{3,2,1,0:T(8,128)} convert(bf16[2,9,8,2560]{3,2,1,0:T(8,128)(2,1)S(1)} %bitcast.6) | non-fusion elementwise | flops 368640 | bytes 2211840 | tf_op jit(solution)/shard_map/reshape | solution.py:293
  3.8 26.3 %shard_map.55 = (bf16[8,384,256]{2,1,0:T(8,128)(2,1)}, bf16[2,576,2560]{2,1,0:T(8,128)(2,1)}) custom-call(bf16[16,64,256]{2,1,0:T(8,128)(2,1)} %field_ref.1, f32[2,9,8,2560]{3,2,1,0:T(8,128)} %convert.5.spread_ref), custom_call_target="tpu_custom_call" | custom-call | tf_op jit(solution)/shard_map/pallas_call | solution.py:298
  30.1 28.9 %shard_map.56.in_ref = bf16[8,128,256]{2,1,0:T(8,128)(2,1)} custom-call(s32[2,5]{1,0:T(2,128)} %concatenate.3.shift_ref, bf16[8,384,256]{2,1,0:T(8,128)(2,1)} %get-tuple-element.7.ext_ref, bf16[2,576,2560]{2,1,0:T(8,128)(2,1)} %get-tuple-element.8.weights_ref, bf16[9,32,256]{2,1,0:T(8,128)(2,1)} %mixing_ref.1), custom_call_target="tpu_custom_call" | custom-call | tf_op jit(solution)/shard_map/pallas_call | solution.py:298
  59.0 2.3 %shard_map.57 = bf16[16,64,256]{2,1,0:T(8,128)(2,1)} custom-call(bf16[8,128,256]{2,1,0:T(8,128)(2,1)} %shard_map.56.in_ref), custom_call_target="tpu_custom_call" | custom-call | tf_op jit(solution)/shard_map/pallas_call | solution.py:298

commit v4 on v3

--- a/solution.py
+++ b/solution.py
@@ -55,21 +55,28 @@
     v = lax.broadcasted_iota(jnp.int32, (BW, width), 0)
     lane = lax.broadcasted_iota(jnp.int32, (BW, width), 1)
     u = lane % BW
-    keep_low = jnp.where(lane < SLAB, u - v, -1) >= 0
-    keep_high = jnp.where(lane < SLAB, -1, v - u - 1) >= 0
+    score = jnp.where(lane < SLAB, u - v, v - u - 1)
+    keep = score >= 0
+    keep_first = jnp.where(lane // BW == TALL - 1, -1, score) >= 0
+    keep_last = jnp.where(lane // BW == TALL, -1, score) >= 0
 
     def body(index, carry):
         group, k = index // K, index % K
         rows = spread_ref[group, k]
+        placed = []
+        for b in range(NB):
+            taps = rows[:, b * width : (b + 1) * width]
+            low = pltpu.roll(taps, 0, 1, stride=BW, stride_axis=0)
+            high = pltpu.roll(taps, SLAB - BW, 1, stride=BW, stride_axis=0)
+            placed.append(low + high)
         blocks = []
         for p in range(RG):
+            kept = {0: keep_first, RG - 1: keep_last}.get(p, keep)
             pieces = []
             for b in range(NB):
-                row = rows[p : p + 1, b * width : (b + 1) * width]
-                wide = jnp.broadcast_to(row, (BW, width))
-                low = pltpu.roll(wide, BW * p, 1, stride=1, stride_axis=0)
-                high = pltpu.roll(wide, SLAB - BW + BW * p, 1, stride=1, stride_axis=0)
-                pieces.append(jnp.where(keep_low, low, jnp.where(keep_high, high, 0.0)))
+                wide = jnp.broadcast_to(placed[b][p : p + 1], (BW, width))
+                turned = pltpu.roll(wide, 0, 1, stride=1, stride_axis=0)
+                pieces.append(jnp.where(kept, turned, 0.0))
             blocks.append(jnp.concatenate(pieces, axis=1))
         tall = jnp.concatenate(blocks, axis=0).astype(jnp.bfloat16)
         out_ref[group, pl.ds(pl.multiple_of(k * RG * BW, RG * BW), RG * BW), :] = tall

time: 61.6 us -> 62.1 us (level)
  no operation moved by 1% of the time
where the time goes in v4:
time: 62.1 us; the launch traced here: 61.9 us
  Pallas kernels  58 us (93%)
  other arithmetic  2.11 us (3%)
  local copies, waits for them, and re-layouts  1.7 us (3%)
    pallas_call x3, Pallas kernels, call(): pl.pallas_call(kernel, out_shape=[jax.ShapeDtypeStruct(shape, jnp.bfloat1...  58 us
    reshape x1, other arithmetic, spread_filters(): return f.reshape(groups, K, RG, NB * 2 * SLAB)  1.36 us

profile of v4, /device:TPU:1, one launch (start us, length us, event | category | flops | bytes accessed | tf_op | source)
XLA Modules:
  0.0 61.9 jit_solution(9655548793022102043)
XLA Ops:
  0.0 0.8 %broadcast_multiply_fusion = s32[2,4]{1,0:T(2,128)S(1)} fusion(s32[2,4]{1,0:T(2,128)} %param.8, s32[2]{0:T(128)} %param.7), kind=kLoop, calls=%fused_computation.1 | loop fusion | flops 8 | bytes 72 | tf_op jit(solution)/shard_map/mul | solution.py:344
  0.8 0.6 concatenate.3.shift_ref
  1.3 1.1 %copy.8 = bf16[2,8,4,9,264]{4,1,2,3,0:T(8,128)(2,1)S(1)} copy(bf16[2,8,4,9,264]{4,2,3,1,0:T(4,128)(2,1)} %bitcast.8) | data formatting | bytes 608256 | tf_op jit(solution)/shard_map/convert_element_type | solution.py:299
  2.4 0.1 pad.6
  2.5 1.4 %convert.5.spread_ref = f32[2,9,8,2560]{3,2,1,0:T(8,128)} convert(bf16[2,9,8,2560]{3,2,1,0:T(8,128)(2,1)S(1)} %bitcast.6) | non-fusion elementwise | flops 368640 | bytes 2211840 | tf_op jit(solution)/shard_map/reshape | solution.py:300
  3.8 26.3 %shard_map.55 = (bf16[8,384,256]{2,1,0:T(8,128)(2,1)}, bf16[2,576,2560]{2,1,0:T(8,128)(2,1)}) custom-call(bf16[16,64,256]{2,1,0:T(8,128)(2,1)} %field_ref.1, f32[2,9,8,2560]{3,2,1,0:T(8,128)} %convert.5.spread_ref), custom_call_target="tpu_custom_call" | custom-call | tf_op jit(solution)/shard_map/pallas_call | solution.py:305
  30.1 29.4 %shard_map.56.in_ref = bf16[8,128,256]{2,1,0:T(8,128)(2,1)} custom-call(s32[2,5]{1,0:T(2,128)} %concatenate.3.shift_ref, bf16[8,384,256]{2,1,0:T(8,128)(2,1)} %get-tuple-element.7.ext_ref, bf16[2,576,2560]{2,1,0:T(8,128)(2,1)} %get-tuple-element.8.weights_ref, bf16[9,32,256]{2,1,0:T(8,128)(2,1)} %mixing_ref.1), custom_call_target="tpu_custom_call" | custom-call | tf_op jit(solution)/shard_map/pallas_call | solution.py:305
  59.5 2.3 %shard_map.57 = bf16[16,64,256]{2,1,0:T(8,128)(2,1)} custom-call(bf16[8,128,256]{2,1,0:T(8,128)(2,1)} %shard_map.56.in_ref), custom_call_target="tpu_custom_call" | custom-call | tf_op jit(solution)/shard_map/pallas_call | solution.py:305

commit v5 on v3

--- a/solution.py
+++ b/solution.py
@@ -60,7 +60,7 @@
 
     def body(index, carry):
         group, k = index // K, index % K
-        rows = spread_ref[group, k]
+        rows = spread_ref[group, k].astype(jnp.float32)
         blocks = []
         for p in range(RG):
             pieces = []
@@ -289,7 +289,7 @@
     groups = rows // RG
     taps = filters.shape[3]
     f = filters.reshape(groups, RG, NB, K, taps).transpose(0, 3, 1, 2, 4)
-    f = jnp.pad(f.astype(jnp.float32), ((0, 0),) * 4 + ((0, 2 * SLAB - taps),))
+    f = jnp.pad(f, ((0, 0),) * 4 + ((0, 2 * SLAB - taps),))
     return f.reshape(groups, K, RG, NB * 2 * SLAB)
 
 

time: 61.6 us -> 60.9 us (0.989)
  other arithmetic: 2.11 us -> 0.75 us
  local copies, waits for them, and re-layouts: 1.7 us -> 2.58 us
    reshape x1 -> x0, other arithmetic: 1.36 us -> none  [spread_filters(): return f.reshape(groups, K, RG, NB * 2 * SLAB)]
    convert_element_type x1 -> x0, local copies, waits for them, and re-layouts: 1.07 us -> none  [spread_filters(): f = jnp.pad(f.astype(jnp.float32), ((0, 0),) * 4 + ((0, 2 * SLAB - taps),))]
    reshape x0 -> x1, local copies, waits for them, and re-layouts: none -> 1.07 us  [spread_filters(): f = filters.reshape(groups, RG, NB, K, taps).transpose(0, 3, 1, 2, 4)]
    pad x1, local copies, waits for them, and re-layouts: 0.07 us -> 0.95 us  [spread_filters(): f = jnp.pad(f, ((0, 0),) * 4 + ((0, 2 * SLAB - taps),))]
where the time goes in v5:
time: 60.9 us; the launch traced here: 60.6 us
  Pallas kernels  57.3 us (94%)
  local copies, waits for them, and re-layouts  2.58 us (4%)
  other arithmetic  0.75 us (1%)
    pallas_call x3, Pallas kernels, call(): pl.pallas_call(kernel, out_shape=[jax.ShapeDtypeStruct(shape, jnp.bfloat1...  57.3 us

profile of v5, /device:TPU:1, one launch (start us, length us, event | category | flops | bytes accessed | tf_op | source)
XLA Modules:
  0.0 60.6 jit_solution(2583600032565102888)
XLA Ops:
  0.0 0.8 %broadcast_multiply_fusion = s32[2,4]{1,0:T(2,128)S(1)} fusion(s32[2,4]{1,0:T(2,128)} %param.8, s32[2]{0:T(128)} %param.7), kind=kLoop, calls=%fused_computation.1 | loop fusion | flops 8 | bytes 72 | tf_op jit(solution)/shard_map/mul | solution.py:337
  0.8 0.6 concatenate.3.shift_ref
  1.3 1.1 %copy.8 = bf16[2,8,4,9,264]{4,1,2,3,0:T(8,128)(2,1)S(1)} copy(bf16[2,8,4,9,264]{4,2,3,1,0:T(4,128)(2,1)} %bitcast.7) | data formatting | bytes 608256 | tf_op jit(solution)/shard_map/reshape | solution.py:291
  2.4 0.9 %pad.5 = bf16[2,9,8,4,640]{4,2,3,1,0:T(8,128)(2,1)} pad(bf16[2,9,8,4,264]{4,2,3,1,0:T(8,128)(2,1)S(1)} %bitcast.6, bf16[]{:T(256)} %constant.19.clone.1), padding=0_0x0_0x0_0x0_0x0_376 | pad | bytes 1041410 | tf_op jit(solution)/shard_map/jit(_pad)/pad | solution.py:292
  3.3 26.0 %shard_map.55 = (bf16[8,384,256]{2,1,0:T(8,128)(2,1)}, bf16[2,576,2560]{2,1,0:T(8,128)(2,1)}) custom-call(bf16[16,64,256]{2,1,0:T(8,128)(2,1)} %field_ref.1, bf16[2,9,8,2560]{3,2,1,0:T(8,128)(2,1)} %bitcast.5), custom_call_target="tpu_custom_call" | custom-call | tf_op jit(solution)/shard_map/pallas_call | solution.py:298
  29.4 28.9 %shard_map.56.in_ref = bf16[8,128,256]{2,1,0:T(8,128)(2,1)} custom-call(s32[2,5]{1,0:T(2,128)} %concatenate.3.shift_ref, bf16[8,384,256]{2,1,0:T(8,128)(2,1)} %get-tuple-element.7.ext_ref, bf16[2,576,2560]{2,1,0:T(8,128)(2,1)} %get-tuple-element.8.weights_ref, bf16[9,32,256]{2,1,0:T(8,128)(2,1)} %mixing_ref.1), custom_call_target="tpu_custom_call" | custom-call | tf_op jit(solution)/shard_map/pallas_call | solution.py:298
  58.3 2.3 %shard_map.57 = bf16[16,64,256]{2,1,0:T(8,128)(2,1)} custom-call(bf16[8,128,256]{2,1,0:T(8,128)(2,1)} %shard_map.56.in_ref), custom_call_target="tpu_custom_call" | custom-call | tf_op jit(solution)/shard_map/pallas_call | solution.py:298
